TPU v7x, 32 devices: a whole 2x2x4 slice. The times are simulated.
32 devices in a mesh: fsdp: 32 (over z, y, x, core), tp: 1.
Axes of the slice: x: 2, y: 2, z: 4, core: 2. Of those that a mesh axis runs over, the one named last changes fastest.
Arguments:
- momentum: float32 [32, 26624], P('fsdp', 'tp'), may hold values from -510 to 510
- gradient: float32 [32, 26624], P('fsdp', 'tp'), may hold values from -6 to 6
- basis: float32 [2, 26624], P(None, 'tp'), may hold values from -0.0390625 to 0.0390625
- weight: bfloat16 [32, 26624], P('fsdp', 'tp'), may hold values from -1 to 1
- inputs: bfloat16 [4096, 32], P('fsdp'), may hold values from -6 to 6
Outputs:
- new_momentum: float32 [32, 26624], P('fsdp', 'tp')
- new_basis: float32 [2, 26624], P(None, 'tp')
- new_weight: bfloat16 [32, 26624], P('fsdp', 'tp')
- activations: bfloat16 [4096, 26624], P('fsdp', 'tp')
All inputs are finite; a program needn't handle non-finite values.
Results may differ from a plain program's by a relative error of at most 0.0049.
Values may be sent and summed in bfloat16 or wider, within the bound.
A program may use at most 64 MiB of HBM per device.

v0:
```python
import math

import jax
import jax.numpy as jnp
from jax import lax
from jax.sharding import PartitionSpec as P

decay_rate = 0.8
step_size = 0.5
epsilon = 1e-06
highest = lax.Precision.HIGHEST


def product(left, right):
    return jnp.dot(left, right, precision=highest, preferred_element_type=jnp.float32)


def contract_rows(left, right):
    return lax.dot_general(
        left, right, (((0,), (0,)), ((), ())), precision=highest, preferred_element_type=jnp.float32
    )


def contract_cols(left, right):
    return lax.dot_general(
        left, right, (((1,), (1,)), ((), ())), precision=highest, preferred_element_type=jnp.float32
    )


def lower_solve(lower, right):
    return lax.linalg.triangular_solve(lower, right, left_side=True, lower=True)


def on_device(momentum, gradient, basis, weight, inputs):
    fsdp_size = lax.axis_size("fsdp")
    tp_size = lax.axis_size("tp")
    rows_local = momentum.shape[0]
    width_local = momentum.shape[1]
    scale = step_size * math.sqrt(width_local * tp_size / (rows_local * fsdp_size))
    buffer = decay_rate * momentum + gradient
    partial_power = contract_cols(buffer, basis)
    power = lax.psum(partial_power, "tp")
    gram, raw_coeff = lax.psum((contract_rows(power, power), contract_rows(power, buffer)), "fsdp")
    lower = jnp.linalg.cholesky(gram)
    ortho = lower_solve(lower, power.T).T
    coeff = lower_solve(lower, raw_coeff)
    squares = lax.psum(jnp.sum(coeff * coeff, axis=1), "tp")
    new_basis = coeff / jnp.sqrt(squares + epsilon)[:, None]
    new_momentum = buffer - (1.0 - decay_rate) * product(ortho, coeff)
    new_weight = (weight.astype(jnp.float32) - scale * product(ortho, new_basis)).astype(
        jnp.bfloat16
    )
    summed = jnp.dot(
        inputs,
        lax.all_gather(new_weight, "fsdp", axis=0, tiled=True),
        preferred_element_type=jnp.float32,
    )
    activations = summed.astype(jnp.bfloat16)
    return (new_momentum, new_basis, new_weight, activations)


def solution(mesh):
    return jax.shard_map(
        on_device,
        mesh=mesh,
        in_specs=(
            P("fsdp", "tp"),
            P("fsdp", "tp"),
            P(None, "tp"),
            P("fsdp", "tp"),
            P("fsdp", None),
        ),
        out_specs=(P("fsdp", "tp"), P(None, "tp"), P("fsdp", "tp"), P("fsdp", "tp")),
        check_vma=False,
    )
```

profile of v0, /device:TPU:0, one launch (start us, length us, event | category | flops | bytes accessed | tf_op | source)
XLA Modules:
  0.0 229.1 jit_solution(16099016919062906767)
XLA Ops:
  7.2 0.0 all-reduce.2.cloned.1.call-start
  7.2 1.1 multiply_add_fusion
  8.4 2.0 fusion.3
  10.4 0.1 broadcast_multiply_fusion.3
  10.5 0.8 broadcast_multiply_fusion
  11.4 0.0 all-reduce.2.cloned.1.call-update
  11.4 0.0 all-gather.3.cloned.1.call-start
  11.4 42.0 %psum.14 = f32[2,2]{0,1:T(2,128)S(1)} all-reduce(f32[2,2]{0,1:T(2,128)S(1)} %broadcast_multiply_fusion.3), channel_id=1, replica_groups=mesh['fsdp'=32,'tp'=1] {'fsdp'}, use_global_device_ids=true, to_apply=%region_0.0 | all-reduce | flops 4 | bytes 32 | tf_op jit(solution)/shard_map/psum | solution.py:43
  53.5 0.1 copy.15
  53.6 0.2 cholesky.16
  53.8 0.6 compare_reduce_fusion
  54.4 0.6 fusion.5
  55.1 0.2 custom-call.8
  55.3 0.1 convolution_bitcast_fusion
  55.4 84.5 %all-reduce.2.cloned.1.call-done = f32[2,26624]{1,0:T(2,128)} async-done(((f32[2,26624]{1,0:T(2,128)}), f32[2,26624]{1,0:T(2,128)}) %all-reduce.2.cloned.1.call-update) | async-done | bytes 213008 | tf_op jit(solution)/shard_map/psum | solution.py:43
  139.9 2.1 multiply_reduce_fusion
  142.0 0.2 broadcast_divide_fusion
  142.2 0.8 fusion.13
  143.1 1.7 subtract_convert_fusion
  144.8 0.8 fusion.12
  145.7 0.8 sub.6
  146.4 59.2 %all-gather.3.cloned.1.call-done = bf16[32,1,26624]{2,1,0:T(2,128)(2,1)} async-done(((bf16[1,1,26624]{2,1,0:T(2,128)(2,1)}), bf16[32,1,26624]{2,1,0:T(2,128)(2,1)}) %all-gather.3.cloned.1.call-update) | async-done | bytes 1703952 | tf_op jit(solution)/shard_map/all_gather | solution.py:55
  205.6 6.8 %fusion = bf16[128,26624]{0,1:T(8,128)(2,1)} fusion(bf16[128,32]{0,1:T(8,128)(2,1)S(1)} %copy-done.2, bf16[32,1,26624]{2,1,0:T(2,128)(2,1)} %all-gather.3.cloned.1.call-done), kind=kOutput, calls=%fused_computation.1 | convolution fusion | flops 221511680 | bytes 8527872 | tf_op jit(solution)/shard_map/dot_general | solution.py:53
  212.4 9.9 %copy.17 = bf16[128,26624]{1,0:T(8,128)(2,1)} copy(bf16[128,26624]{0,1:T(8,128)(2,1)} %fusion) | data formatting | bytes 13631488
  (12 shorter events, 0.1 us)
Async XLA Ops:
  7.2 1.2 copy-start
  7.2 198.4 %copy-start.2 = (bf16[128,32]{0,1:T(8,128)(2,1)S(1)}, bf16[128,32]{0,1:T(8,128)(2,1)}, u32[]{:S(2)}) copy-start(bf16[128,32]{0,1:T(8,128)(2,1)} %param.9) | copy-start | bytes 24580
  7.2 132.7 %all-reduce.2.cloned.1.call-start = ((), (), s32[]{:S(2)}) async-start(), calls=%async_computation | async-start | bytes 425984 | tf_op jit(solution)/shard_map/psum | solution.py:43
  11.4 194.2 %all-gather.3.cloned.1.call-start = ((), (), s32[]{:S(2)}) async-start(), calls=%async_computation.1 | async-start | bytes 3514368 | tf_op jit(solution)/shard_map/all_gather | solution.py:55
  142.2 70.2 %copy-start.1 = (f32[2,26624]{1,0:T(2,128)}, f32[2,26624]{1,0:T(2,128)S(1)}, u32[]{:S(2)}) copy-start(f32[2,26624]{1,0:T(2,128)S(1)} %broadcast_divide_fusion) | copy-start | bytes 638980
Sparse Core Ops, SparseCore 0:
  14.1 125.7 all-reduce.1
  144.9 60.6 all-gather.2
where the time goes:
time: 230 us; the launch traced here: 229 us
  waiting for transfers between devices  144 us (63%)
  blocking collectives  42 us (18%)
  between operations  14.1 us (6%)
  matrix products  12.8 us (6%)
  local copies, waits for them, and re-layouts  10 us (4%)
  other arithmetic  6.39 us (3%)
    psum x1, waiting for transfers between devices, on_device(): lax.psum((contract_rows(power, power), contract_rows(power, buffer)), 'fs...  84.5 us
    all_gather x1, waiting for transfers between devices, on_device(): lax.all_gather(new_weight, 'fsdp', axis=0, tiled=True)  59.2 us
    psum x1, blocking collectives, on_device(): lax.psum((contract_rows(power, power), contract_rows(power, buffer)), 'fs...  42 us
    unnamed x7, local copies, waits for them, and re-layouts  9.93 us
    dot_general x1, matrix products, on_device(): jnp.dot(inputs, lax.all_gather(new_weight, 'fsdp', axis=0, tiled=True), p...  6.76 us
  transfers between devices with their start and end apart: 2, of which 2 were waited for; matrix products, arithmetic and copies ran while one was open for 2% of the time, Pallas kernels for 0%

commit v1 on v0

v1 whole, which is shorter than its diff:
```python
import functools
import math

import jax
import jax.numpy as jnp
from jax import lax
from jax.experimental import pallas as pl
from jax.experimental.pallas import tpu as pltpu
from jax.sharding import PartitionSpec as P

decay_rate = 0.8
step_size = 0.5
epsilon = 1e-06
highest = lax.Precision.HIGHEST
MESH = pl.DeviceIdType.MESH
LANES = 128
CHUNK = 16
SUB = 8

BUFFER_PLAN = (("yzx", 4), ("xzy", 4), ("zxy", 3), ("zyx", 2))
WEIGHT_PLAN = (("yzx", 4), ("xzy", 4), ("zxy", 3), ("zyx", 2))


def split_chunks(plan, chunks):
    total = sum(share for _, share in plan)
    parts, start, seen = [], 0, 0
    for order, share in plan:
        seen += share
        stop = (chunks * seen) // total
        if stop > start:
            parts.append((order, start, stop - start))
        start = stop
    return parts


class Mover:
    def __init__(self, buf, window, order, number, coords, depth, send_sem, recv_sem):
        self.buf, self.window, self.order, self.number = buf, window, order, number
        self.coords, self.depth = coords, depth
        self.send_sem, self.recv_sem = send_sem, recv_sem
        self.sent = []
        self.phase = 0

    def block(self, **fixed):
        done = self.order[: self.phase]
        index = []
        for axis in "zyxc":
            if axis in fixed:
                index.append(fixed[axis])
            elif axis in done:
                index.append(slice(None))
            else:
                index.append(self.coords[axis])
        return self.buf.at[tuple(index) + self.window]

    def copy(self, ref, slot, **target):
        where = dict(self.coords, **target)
        device = ((where["z"] * 2 + where["y"]) * 2 + where["x"]) * 2 + where["c"]
        return pltpu.make_async_remote_copy(
            src_ref=ref,
            dst_ref=ref,
            send_sem=self.send_sem.at[self.number, slot],
            recv_sem=self.recv_sem.at[self.number, slot],
            device_id={"fsdp": device},
            device_id_type=MESH,
        )

    def hops(self):
        axis = self.order[self.phase]
        base = self.order.index(axis) if axis != "z" else 4
        if axis == "z":
            return [(4 + k, (self.coords["z"] + k) % self.depth, (self.coords["z"] + self.depth - k) % self.depth)
                    for k in range(1, self.depth)]
        other = 1 - self.coords[axis]
        return [(base if base < 2 else 2, other, other)]

    def start(self):
        axis = self.order[self.phase]
        for slot, target, _ in self.hops():
            copy = self.copy(self.block(), slot, **{axis: target})
            copy.start()
            self.sent.append(copy)

    def finish(self):
        axis = self.order[self.phase]
        for slot, _, source in self.hops():
            self.copy(self.block(**{axis: source}), slot, **{axis: source}).wait_recv()
        self.phase += 1

    def to_sibling(self, last):
        axis = self.order[2]
        side = 1 - self.coords[axis] if last else self.coords[axis]
        copy = self.copy(self.block(**{axis: side}), 3 if last else 4, c=1 - self.coords["c"])
        copy.start()
        self.sent.append(copy)

    def from_sibling(self):
        axis, other = self.order[2], 1 - self.coords["c"]
        for side, slot in ((self.coords[axis], 4), (1 - self.coords[axis], 3)):
            self.copy(self.block(**{axis: side, "c": other}), slot, c=other).wait_recv()

    def drain(self):
        for copy in self.sent:
            copy.wait_send()


def gather_kernel(depth, rank, rows_local, has_power, *refs):
    (m_ref, g_ref, basis_ref, w_ref, power_ref, gathered, coeff_ref, ortho_ref, mine_ref, squares_ref,
     rows_buf, power_buf, send_sem, recv_sem, local_sem) = refs
    chunks = m_ref.shape[1] // CHUNK
    me = lax.axis_index("fsdp")
    coords = {"z": me // 8, "y": (me // 4) % 2, "x": (me // 2) % 2, "c": me % 2}
    here = (coords["z"], coords["y"], coords["x"], coords["c"])

    def number(z, y, x, c):
        return ((z * 2 + y) * 2 + x) * 2 + c

    partners = [number((coords["z"] + k) % depth, *here[1:]) for k in range(1, depth)]
    partners += [
        number(here[0], 1 - here[1], here[2], here[3]),
        number(here[0], here[1], 1 - here[2], here[3]),
        number(here[0], here[1], here[2], 1 - here[3]),
    ]
    barrier = pltpu.get_barrier_semaphore()
    for partner in partners:
        pl.semaphore_signal(barrier, inc=1, device_id={"fsdp": partner}, device_id_type=MESH)

    own = pltpu.make_async_copy(w_ref, gathered.at[here], local_sem)
    own.start()

    for row in range(rows_local):
        buffer = decay_rate * m_ref[row] + g_ref[row]
        rows_buf[here + (row,)] = buffer.astype(jnp.bfloat16)
        if has_power:
            power_buf[here + (pl.ds(row * SUB, SUB),)] = power_ref[pl.ds(row * SUB, SUB)]
        else:
            tile = [
                jnp.broadcast_to(
                    jnp.sum(buffer * basis_ref[pl.ds(k, m_ref.shape[1], stride=rank)], keepdims=True), (1, LANES)
                )
                for k in range(rank)
            ]
            tile += [jnp.zeros((1, LANES), jnp.float32)] * (SUB - rank)
            power_buf[here + (pl.ds(row * SUB, SUB),)] = jnp.concatenate(tile, axis=0)
    pl.semaphore_wait(barrier, len(partners))

    def mover(buf, window, order, count):
        return Mover(buf, window, order, count, coords, depth, send_sem, recv_sem)

    def windows(plan):
        return [
            (order, (slice(None), pl.ds(first * CHUNK, count * CHUNK), slice(None)))
            for order, first, count in split_chunks(plan, chunks)
        ]

    early = [mover(power_buf, (slice(None), slice(None)), "zxy", 0)]
    for order, window in windows(BUFFER_PLAN):
        early.append(mover(rows_buf, window, order, len(early)))
    late = []
    for order, window in windows(WEIGHT_PLAN):
        late.append(mover(gathered, window, order, len(early) + len(late)))

    def advance(movers):
        for part in movers:
            part.finish()
            if part.phase == 2:
                part.to_sibling(False)
            if part.phase < 3:
                part.start()
            else:
                part.to_sibling(True)

    for part in early:
        part.start()
    own.wait()
    for part in late:
        part.start()
    advance(early)
    advance(late)
    advance(early)
    advance(late)
    advance(early)
    for part in early:
        part.from_sibling()

    devices = [(z, y, x, c) for z in range(depth) for y in range(2) for x in range(2) for c in range(2)]
    tiles = [power_buf[d + (pl.ds(row * SUB, SUB),)] for d in devices for row in range(rows_local)]
    gram = []
    for l in range(rank):
        total = jnp.zeros((SUB, LANES), jnp.float32)
        for tile in tiles:
            total = total + tile * tile[l : l + 1]
        gram.append(total)
    lower = [[None] * rank for _ in range(rank)]
    inverse = [None] * rank
    for l in range(rank):
        value = gram[l][l : l + 1]
        for j in range(l):
            value = value - lower[l][j] * lower[l][j]
        lower[l][l] = jnp.sqrt(value)
        inverse[l] = 1.0 / lower[l][l]
        for k in range(l + 1, rank):
            value = gram[l][k : k + 1]
            for j in range(l):
                value = value - lower[k][j] * lower[l][j]
            lower[k][l] = value * inverse[l]

    def solve(right):
        found = []
        for k in range(rank):
            value = right[k]
            for j in range(k):
                value = value - lower[k][j] * found[j]
            found.append(value * inverse[k])
        return found

    filler = [jnp.zeros((1, LANES), jnp.float32)] * (SUB - rank)
    for i, tile in enumerate(tiles):
        found = solve([tile[k : k + 1] for k in range(rank)])
        ortho_ref[pl.ds(i * SUB, SUB)] = jnp.concatenate(found + filler, axis=0)
    for row in range(rows_local):
        tile = power_buf[here + (pl.ds(row * SUB, SUB),)]
        found = solve([tile[k : k + 1] for k in range(rank)])
        mine_ref[pl.ds(row * SUB, SUB)] = jnp.concatenate(found + filler, axis=0)

    def one_chunk(i, squares):
        at = pl.ds(pl.multiple_of(i * CHUNK, CHUNK), CHUNK)
        raw = [jnp.zeros((CHUNK, LANES), jnp.float32) for _ in range(rank)]
        for d in devices:
            for row in range(rows_local):
                values = rows_buf[d + (row, at)].astype(jnp.float32)
                for k in range(rank):
                    raw[k] = raw[k] + values * power_buf[d + (pl.ds(row * SUB + k, 1),)]
        found = solve(raw)
        for k in range(rank):
            coeff_ref[k, at] = found[k]
        return tuple(squares[k] + found[k] * found[k] for k in range(rank))

    squares = lax.fori_loop(
        0, chunks, one_chunk, tuple(jnp.zeros((CHUNK, LANES), jnp.float32) for _ in range(rank))
    )
    squares_ref[...] = jnp.concatenate(
        [jnp.broadcast_to(jnp.sum(squares[k], keepdims=True), (1, LANES)) for k in range(rank)] + filler, axis=0
    )

    advance(late)
    for part in late:
        part.from_sibling()
    for part in early + late:
        part.drain()


def apply_kernel(scale, rank, rows_local, ortho_ref, mine_ref, squares_ref, x_ref, w_all_ref, coeff_ref, m_ref, g_ref,
                 w_ref, act_ref, nm_ref, nb_ref, nw_ref, spread):
    rows = w_all_ref.shape[0]
    coeff = [coeff_ref[k] for k in range(rank)]
    basis = []
    for k in range(rank):
        norm = jnp.sqrt(squares_ref[k : k + 1] + epsilon)
        basis.append(coeff[k] * (1.0 / norm))
        nb_ref[pl.ds(k, CHUNK, stride=rank)] = basis[k]

    def lowered(weight, ref, row):
        change = ref[pl.ds(row * SUB, 1)] * basis[0]
        for k in range(1, rank):
            change = change + ref[pl.ds(row * SUB + k, 1)] * basis[k]
        return weight.astype(jnp.float32) - scale * change

    for row in range(rows_local):
        nw_ref[row] = lowered(w_ref[row], mine_ref, row).astype(jnp.bfloat16)
        feedback = mine_ref[pl.ds(row * SUB, 1)] * coeff[0]
        for k in range(1, rank):
            feedback = feedback + mine_ref[pl.ds(row * SUB + k, 1)] * coeff[k]
        nm_ref[row] = decay_rate * m_ref[row] + g_ref[row] - (1.0 - decay_rate) * feedback
    for row in range(rows):
        spread[pl.ds(row * CHUNK, CHUNK)] = lowered(w_all_ref[row], ortho_ref, row)
    weights = jnp.concatenate(
        [spread[pl.ds(j, rows, stride=CHUNK)].astype(jnp.bfloat16) for j in range(CHUNK)], axis=1
    )
    act_ref[...] = jnp.dot(x_ref[...], weights, preferred_element_type=jnp.float32).astype(jnp.bfloat16)


def on_device(fsdp, tp, momentum, gradient, basis, weight, inputs):
    rows_local, width = momentum.shape
    rank = basis.shape[0]
    rows = rows_local * fsdp
    tokens = inputs.shape[0]
    depth = fsdp // 8
    assert depth * 8 == fsdp and rank <= SUB
    scale = step_size * math.sqrt(width * tp / rows)
    block = CHUNK * LANES
    padded = -(-width // block) * block
    groups = padded // LANES
    chunks = groups // CHUNK

    def dense(array):
        if padded != width:
            array = jnp.pad(array, ((0, 0), (0, padded - width)))
        return array.reshape(array.shape[0], groups, LANES)

    m, g, w = dense(momentum), dense(gradient), dense(weight)
    b = dense(basis).transpose(1, 0, 2).reshape(groups * rank, LANES)
    if tp > 1:
        buffer = decay_rate * momentum + gradient
        power = lax.psum(
            lax.dot_general(buffer, basis, (((1,), (1,)), ((), ())), precision=highest,
                            preferred_element_type=jnp.float32), "tp")
        power = jnp.pad(power, ((0, 0), (0, SUB - rank))).reshape(rows_local * SUB, 1)
        power = jnp.broadcast_to(power, (rows_local * SUB, LANES))
    else:
        power = jnp.zeros((SUB, LANES), jnp.float32)

    vmem = pl.BlockSpec(memory_space=pltpu.VMEM)
    anywhere = pl.BlockSpec(memory_space=pl.ANY)
    parts = 1 + len(split_chunks(BUFFER_PLAN, chunks)) + len(split_chunks(WEIGHT_PLAN, chunks))
    f32, bf16 = jnp.float32, jnp.bfloat16
    gathered, coeff, ortho, mine, squares = pl.pallas_call(
        functools.partial(gather_kernel, depth, rank, rows_local, tp > 1),
        out_shape=(
            jax.ShapeDtypeStruct((depth, 2, 2, 2, rows_local, groups, LANES), bf16),
            jax.ShapeDtypeStruct((rank, groups, LANES), f32),
            jax.ShapeDtypeStruct((rows * SUB, LANES), f32),
            jax.ShapeDtypeStruct((rows_local * SUB, LANES), f32),
            jax.ShapeDtypeStruct((SUB, LANES), f32),
        ),
        in_specs=[vmem] * 5,
        out_specs=(anywhere, vmem, vmem, vmem, vmem),
        scratch_shapes=[
            pltpu.VMEM((depth, 2, 2, 2, rows_local, groups, LANES), bf16),
            pltpu.VMEM((depth, 2, 2, 2, rows_local * SUB, LANES), f32),
            pltpu.SemaphoreType.DMA((parts, 4 + depth)),
            pltpu.SemaphoreType.DMA((parts, 4 + depth)),
            pltpu.SemaphoreType.DMA,
        ],
        compiler_params=pltpu.CompilerParams(
            collective_id=0, has_side_effects=True, vmem_limit_bytes=32 * 1024 * 1024
        ),
        name="gather_rows",
    )(m, g, b, w, power)

    if tp > 1:
        squares = lax.psum(squares, "tp")
    w_all = gathered.reshape(rows, groups, LANES)

    def whole(array):
        return pl.BlockSpec(array.shape, lambda i: (0,) * array.ndim)

    def sliced(lead):
        return pl.BlockSpec((lead, CHUNK, LANES), lambda i: (0, i, 0))

    act, nm, nb, nw = pl.pallas_call(
        functools.partial(apply_kernel, scale, rank, rows_local),
        grid=(chunks,),
        out_shape=(
            jax.ShapeDtypeStruct((tokens, padded), bf16),
            jax.ShapeDtypeStruct((rows_local, groups, LANES), f32),
            jax.ShapeDtypeStruct((groups * rank, LANES), f32),
            jax.ShapeDtypeStruct((rows_local, groups, LANES), bf16),
        ),
        in_specs=[
            whole(ortho), whole(mine), whole(squares), whole(inputs),
            sliced(rows), sliced(rank), sliced(rows_local), sliced(rows_local), sliced(rows_local),
        ],
        out_specs=(
            pl.BlockSpec((tokens, block), lambda i: (0, i)),
            sliced(rows_local),
            pl.BlockSpec((CHUNK * rank, LANES), lambda i: (i, 0)),
            sliced(rows_local),
        ),
        scratch_shapes=[pltpu.VMEM((rows * CHUNK, LANES), f32)],
        compiler_params=pltpu.CompilerParams(vmem_limit_bytes=32 * 1024 * 1024),
        name="apply_update",
    )(ortho, mine, squares, inputs, w_all, coeff, m, g, w)

    def flat(array):
        return array.reshape(array.shape[0], padded)[:, :width]

    new_basis = flat(nb.reshape(groups, rank, LANES).transpose(1, 0, 2))
    return flat(nm), new_basis, flat(nw), act[:, :width]


def solution(mesh):
    return jax.shard_map(
        functools.partial(on_device, mesh.shape["fsdp"], mesh.shape["tp"]),
        mesh=mesh,
        in_specs=(
            P("fsdp", "tp"),
            P("fsdp", "tp"),
            P(None, "tp"),
            P("fsdp", "tp"),
            P("fsdp", None),
        ),
        out_specs=(P("fsdp", "tp"), P(None, "tp"), P("fsdp", "tp"), P("fsdp", "tp")),
        check_vma=False,
    )
```

time: 230 us -> 45.6 us (0.20)
  waiting for transfers between devices: 144 us -> 0 us
  blocking collectives: 42 us -> 0 us
  Pallas kernels: 0 us -> 39.2 us
  between operations: 14.1 us -> 0.66 us
  matrix products: 12.8 us -> 0 us
  local copies, waits for them, and re-layouts: 10 us -> 4.26 us
  other arithmetic: 6.39 us -> 1.19 us
    psum x1 -> x0, waiting for transfers between devices: 84.5 us -> none  [on_device(): lax.psum((contract_rows(power, power), contract_rows(power, buffer)), 'fs...]
    all_gather x1 -> x0, waiting for transfers between devices: 59.2 us -> none  [on_device(): lax.all_gather(new_weight, 'fsdp', axis=0, tiled=True)]
    psum x1 -> x0, blocking collectives: 42 us -> none  [on_device(): lax.psum((contract_rows(power, power), contract_rows(power, buffer)), 'fs...]
    pallas_call x0 -> x2, Pallas kernels: none -> 39.2 us  [the longest x1 31 us: on_device(): pl.pallas_call(functools.partial(gather_kernel, depth, rank, rows_local,...]
    dot_general x4 -> x0, matrix products: 10.5 us -> none  [the longest x1 6.76 us: on_device(): jnp.dot(inputs, lax.all_gather(new_weight, 'fsdp', axis=0, tiled=True), p...]
    unnamed x7 -> x8, local copies, waits for them, and re-layouts: 9.93 us -> 4.25 us
  transfers between devices with their start and end apart: 2 -> 0, of which waited for: 2 -> 0; matrix products, arithmetic and copies ran while one was open for 2% -> 0% of each run, Pallas kernels for 0% -> 0%
where the time goes in v1:
time: 45.6 us; the launch traced here: 45.4 us
  Pallas kernels  39.2 us (86%)
  local copies, waits for them, and re-layouts  4.26 us (9%)
  other arithmetic  1.19 us (3%)
  between operations  0.66 us (1%)
    pallas_call x1, Pallas kernels, on_device(): pl.pallas_call(functools.partial(gather_kernel, depth, rank, rows_local,...  31 us
    pallas_call x1, Pallas kernels, on_device(): pl.pallas_call(functools.partial(apply_kernel, scale, rank, rows_local),...  8.24 us
    unnamed x8, local copies, waits for them, and re-layouts  4.25 us
    unnamed x1, other arithmetic  1.19 us

profile of v1, /device:TPU:0, one launch (start us, length us, event | category | flops | bytes accessed | tf_op | source)
XLA Modules:
  0.0 45.4 jit_solution(15558323286952247761)
XLA Ops:
  0.6 0.8 %copy.10.x_ref = bf16[128,32]{1,0:T(8,128)(2,1)S(1)} copy(bf16[128,32]{0,1:T(8,128)(2,1)} %param.9) | data formatting | bytes 16384 | tf_op args[4]
  1.4 1.2 %reduce = bf16[26624]{0:T(1024)(128)(2,1)S(1)} reduce(bf16[1,26624]{1,0:T(2,128)(2,1)} %param.8, bf16[]{:T(256)} %constant.5), dimensions={0}, to_apply=%param.8.reduce_sub_computation | reduce | bytes 106498 | tf_op args[3]
  2.6 0.0 copy-start
  2.7 0.9 %copy-done = f32[1,26624]{1,0:T(1,128)S(1)} copy-done((f32[1,26624]{1,0:T(1,128)S(1)}, f32[1,26624]{1,0:T(1,128)}, u32[]{:S(2)}) %copy-start) | copy-done | bytes 106520
  3.5 0.0 copy-start.1
  3.5 0.9 %copy-done.1 = f32[1,26624]{1,0:T(1,128)S(1)} copy-done((f32[1,26624]{1,0:T(1,128)S(1)}, f32[1,26624]{1,0:T(1,128)}, u32[]{:S(2)}) %copy-start.1) | copy-done | bytes 106520
  4.4 0.0 copy-start.2
  4.4 0.9 %copy-done.2 = f32[2,26624]{1,0:T(2,128)S(1)} copy-done((f32[2,26624]{1,0:T(2,128)S(1)}, f32[2,26624]{1,0:T(2,128)}, u32[]{:S(2)}) %copy-start.2) | copy-done | bytes 213016
  5.4 31.0 %gather_rows.1 = (bf16[4,2,2,2,1,208,128]{6,5,4,3,2,1,0:T(8,128)(2,1)S(1)}, f32[2,208,128]{2,1,0:T(8,128)S(1)}, f32[256,128]{1,0:T(8,128)S(1)}, f32[8,128]{1,0:T(8,128)S(1)}, f32[8,128]{1,0:T(8,128)S(1)}) custom-call(f32[1,208,128]{2,1,0:T(8,128)S(1)} %bitcast.22, f32[1,208,128]{2,1,0:T(8,128)S(1)} %bitcast.24, f32[416,128]{1,0:T(8,128)S(1)} %bitcast.26, ...), custom_call_target="tpu_custom_call" | custom-call | tf_op jit(solution)/shard_map/gather_rows/pallas_call | solution.py:317
  36.4 8.2 %apply_update.1 = (bf16[128,26624]{1,0:T(8,128)(2,1)}, f32[1,208,128]{2,1,0:T(8,128)}, f32[416,128]{1,0:T(8,128)}, bf16[1,208,128]{2,1,0:T(8,128)(2,1)S(1)}) custom-call(f32[256,128]{1,0:T(8,128)S(1)} %get-tuple-element.13.ortho_ref, f32[8,128]{1,0:T(8,128)S(1)} %get-tuple-element.14.mine_ref, f32[8,128]{1,0:T(8,128)S(1)} %get-tuple-element.15.squares_ref, ...), custom_call_target="tpu_custom_call" | custom-call | tf_op jit(solution)/shard_map/apply_update/pallas_call | solution.py:351
  44.6 0.7 %copy.14 = bf16[1,1,208,128]{3,1,2,0:T(2,128)(2,1)} copy(bf16[1,1,208,128]{3,2,1,0:T(8,128)(2,1)S(1)} %bitcast.27) | data formatting | bytes 106496
  (1 shorter events, 0.0 us)
Async XLA Ops:
  2.6 0.9 %copy-start = (f32[1,26624]{1,0:T(1,128)S(1)}, f32[1,26624]{1,0:T(1,128)}, u32[]{:S(2)}) copy-start(f32[1,26624]{1,0:T(1,128)} %param.5) | copy-start | bytes 319492
  3.5 0.9 %copy-start.1 = (f32[1,26624]{1,0:T(1,128)S(1)}, f32[1,26624]{1,0:T(1,128)}, u32[]{:S(2)}) copy-start(f32[1,26624]{1,0:T(1,128)} %param.6) | copy-start | bytes 319492
  4.4 0.9 %copy-start.2 = (f32[2,26624]{1,0:T(2,128)S(1)}, f32[2,26624]{1,0:T(2,128)}, u32[]{:S(2)}) copy-start(f32[2,26624]{1,0:T(2,128)} %param.7) | copy-start | bytes 638980

commit v2 on v1

--- a/solution.py
+++ b/solution.py
@@ -15,9 +15,9 @@
 MESH = pl.DeviceIdType.MESH
 LANES = 128
 CHUNK = 16
+PITCH = 24
 SUB = 8
 
-BUFFER_PLAN = (("yzx", 4), ("xzy", 4), ("zxy", 3), ("zyx", 2))
 WEIGHT_PLAN = (("yzx", 4), ("xzy", 4), ("zxy", 3), ("zyx", 2))
 
 
@@ -104,10 +104,12 @@
             copy.wait_send()
 
 
-def gather_kernel(depth, rank, rows_local, has_power, *refs):
-    (m_ref, g_ref, basis_ref, w_ref, power_ref, gathered, coeff_ref, ortho_ref, mine_ref, squares_ref,
-     rows_buf, power_buf, send_sem, recv_sem, local_sem) = refs
-    chunks = m_ref.shape[1] // CHUNK
+def gather_kernel(depth, rank, rows_local, unit, has_power, *refs):
+    (m_hbm, g_hbm, basis_hbm, xt_hbm, w_ref, power_ref, gathered, coeff_ref, buffer_ref, x_ref, ortho_ref, mine_ref,
+     squares_ref, m_ref, g_ref, basis_ref, xt_ref, sums, from_c, from_x, from_y, from_z, coeff_buf, power_buf,
+     send_sem, recv_sem, sums_send, sums_recv, local_sem) = refs
+    groups = m_ref.shape[1]
+    chunks = groups // CHUNK
     me = lax.axis_index("fsdp")
     coords = {"z": me // 8, "y": (me // 4) % 2, "x": (me // 2) % 2, "c": me % 2}
     here = (coords["z"], coords["y"], coords["x"], coords["c"])
@@ -116,49 +118,64 @@
         return ((z * 2 + y) * 2 + x) * 2 + c
 
     partners = [number((coords["z"] + k) % depth, *here[1:]) for k in range(1, depth)]
-    partners += [
-        number(here[0], 1 - here[1], here[2], here[3]),
-        number(here[0], here[1], 1 - here[2], here[3]),
-        number(here[0], here[1], here[2], 1 - here[3]),
-    ]
+    over_y = number(here[0], 1 - here[1], here[2], here[3])
+    over_x = number(here[0], here[1], 1 - here[2], here[3])
+    sibling = number(here[0], here[1], here[2], 1 - here[3])
+    partners += [over_y, over_x, sibling]
     barrier = pltpu.get_barrier_semaphore()
     for partner in partners:
         pl.semaphore_signal(barrier, inc=1, device_id={"fsdp": partner}, device_id_type=MESH)
 
-    own = pltpu.make_async_copy(w_ref, gathered.at[here], local_sem)
-    own.start()
+    loads = [
+        pltpu.make_async_copy(source, target, local_sem.at[i])
+        for i, (source, target) in enumerate(
+            ((w_ref, gathered.at[here]), (m_hbm, m_ref), (g_hbm, g_ref), (basis_hbm, basis_ref), (xt_hbm, xt_ref))
+        )
+    ]
+    for load in loads:
+        load.start()
+    for load in loads[1:4]:
+        load.wait()
 
     for row in range(rows_local):
-        buffer = decay_rate * m_ref[row] + g_ref[row]
-        rows_buf[here + (row,)] = buffer.astype(jnp.bfloat16)
+        buffer_ref[row] = decay_rate * m_ref[row] + g_ref[row]
         if has_power:
             power_buf[here + (pl.ds(row * SUB, SUB),)] = power_ref[pl.ds(row * SUB, SUB)]
         else:
             tile = [
                 jnp.broadcast_to(
-                    jnp.sum(buffer * basis_ref[pl.ds(k, m_ref.shape[1], stride=rank)], keepdims=True), (1, LANES)
+                    jnp.sum(buffer_ref[row] * basis_ref[pl.ds(k, groups, stride=rank)], keepdims=True), (1, LANES)
                 )
                 for k in range(rank)
             ]
             tile += [jnp.zeros((1, LANES), jnp.float32)] * (SUB - rank)
             power_buf[here + (pl.ds(row * SUB, SUB),)] = jnp.concatenate(tile, axis=0)
+
+    devices = [(z, y, x, c) for z in range(depth) for y in range(2) for x in range(2) for c in range(2)]
+    owners = groups // unit
+    own_power = [power_buf[here + (pl.ds(row * SUB, SUB),)] for row in range(rows_local)]
+    for i, d in enumerate(devices):
+        for k in range(rank):
+            at = pl.ds(k * unit, unit)
+            if i >= owners:
+                sums[d + (at,)] = jnp.zeros((unit, LANES), jnp.float32)
+                continue
+            term = jnp.zeros((unit, LANES), jnp.float32)
+            for row in range(rows_local):
+                term = term + own_power[row][k : k + 1] * buffer_ref[row, pl.ds(i * unit, unit)]
+            sums[d + (at,)] = term
     pl.semaphore_wait(barrier, len(partners))
 
     def mover(buf, window, order, count):
         return Mover(buf, window, order, count, coords, depth, send_sem, recv_sem)
 
-    def windows(plan):
-        return [
-            (order, (slice(None), pl.ds(first * CHUNK, count * CHUNK), slice(None)))
-            for order, first, count in split_chunks(plan, chunks)
-        ]
-
-    early = [mover(power_buf, (slice(None), slice(None)), "zxy", 0)]
-    for order, window in windows(BUFFER_PLAN):
-        early.append(mover(rows_buf, window, order, len(early)))
+    everything = (slice(None), slice(None))
+    power_part = mover(power_buf, everything, "zxy", 0)
+    coeff_part = mover(coeff_buf, everything, "zxy", 1)
     late = []
-    for order, window in windows(WEIGHT_PLAN):
-        late.append(mover(gathered, window, order, len(early) + len(late)))
+    for order, first, count in split_chunks(WEIGHT_PLAN, chunks):
+        window = (slice(None), pl.ds(first * CHUNK, count * CHUNK), slice(None))
+        late.append(mover(gathered, window, order, 2 + len(late)))
 
     def advance(movers):
         for part in movers:
@@ -170,20 +187,52 @@
             else:
                 part.to_sibling(True)
 
-    for part in early:
-        part.start()
-    own.wait()
+    def sums_copy(source, target, slot, device):
+        return pltpu.make_async_remote_copy(
+            src_ref=source, dst_ref=target, send_sem=sums_send.at[slot], recv_sem=sums_recv.at[slot],
+            device_id={"fsdp": device}, device_id_type=MESH,
+        )
+
+    z, y, x, c = here
+    all_of = slice(None)
+    copy_c = sums_copy(sums.at[all_of, all_of, all_of, 1 - c], from_c, 0, sibling)
+    copy_x = sums_copy(sums.at[all_of, all_of, 1 - x, c], from_x, 1, over_x)
+    copy_y = sums_copy(sums.at[all_of, 1 - y, x, c], from_y, 2, over_y)
+    copy_z = [
+        sums_copy(sums.at[(z + k) % depth, y, x, c], from_z.at[k - 1], 2 + k,
+                  number((z + k) % depth, y, x, c))
+        for k in range(1, depth)
+    ]
+
+    power_part.start()
+    copy_c.start()
+    loads[0].wait()
     for part in late:
         part.start()
-    advance(early)
+    copy_c.wait_recv()
+    for i in range(depth):
+        for j in range(2):
+            for h in range(2):
+                sums[i, j, h, c] = sums[i, j, h, c] + from_c[i, j, h]
+    copy_x.start()
+    advance([power_part])
+    loads[4].wait()
+    x_ref[...] = jnp.transpose(xt_ref[...].astype(jnp.float32)).astype(jnp.bfloat16)
+    copy_x.wait_recv()
+    for i in range(depth):
+        for j in range(2):
+            sums[i, j, x, c] = sums[i, j, x, c] + from_x[i, j]
+    copy_y.start()
+    advance([power_part])
     advance(late)
-    advance(early)
-    advance(late)
-    advance(early)
-    for part in early:
-        part.from_sibling()
-
-    devices = [(z, y, x, c) for z in range(depth) for y in range(2) for x in range(2) for c in range(2)]
+    copy_y.wait_recv()
+    for i in range(depth):
+        sums[i, y, x, c] = sums[i, y, x, c] + from_y[i]
+    for copy in copy_z:
+        copy.start()
+    advance([power_part])
+    power_part.from_sibling()
+
     tiles = [power_buf[d + (pl.ds(row * SUB, SUB),)] for d in devices for row in range(rows_local)]
     gram = []
     for l in range(rank):
@@ -214,43 +263,49 @@
             found.append(value * inverse[k])
         return found
 
+    for copy in copy_z:
+        copy.wait_recv()
+    total = sums[here]
+    for k in range(1, depth):
+        total = total + from_z[k - 1]
+    coeff_buf[here] = jnp.concatenate(solve([total[k * unit : (k + 1) * unit] for k in range(rank)]), axis=0)
+    coeff_part.start()
+
     filler = [jnp.zeros((1, LANES), jnp.float32)] * (SUB - rank)
     for i, tile in enumerate(tiles):
         found = solve([tile[k : k + 1] for k in range(rank)])
         ortho_ref[pl.ds(i * SUB, SUB)] = jnp.concatenate(found + filler, axis=0)
     for row in range(rows_local):
-        tile = power_buf[here + (pl.ds(row * SUB, SUB),)]
+        tile = own_power[row]
         found = solve([tile[k : k + 1] for k in range(rank)])
         mine_ref[pl.ds(row * SUB, SUB)] = jnp.concatenate(found + filler, axis=0)
 
-    def one_chunk(i, squares):
-        at = pl.ds(pl.multiple_of(i * CHUNK, CHUNK), CHUNK)
-        raw = [jnp.zeros((CHUNK, LANES), jnp.float32) for _ in range(rank)]
-        for d in devices:
-            for row in range(rows_local):
-                values = rows_buf[d + (row, at)].astype(jnp.float32)
-                for k in range(rank):
-                    raw[k] = raw[k] + values * power_buf[d + (pl.ds(row * SUB + k, 1),)]
-        found = solve(raw)
+    advance([coeff_part])
+    advance(late)
+    advance([coeff_part])
+    advance([coeff_part])
+    advance(late)
+    coeff_part.from_sibling()
+    squares = [jnp.zeros((unit, LANES), jnp.float32) for _ in range(rank)]
+    for i in range(owners):
+        slot = coeff_buf[devices[i]]
         for k in range(rank):
-            coeff_ref[k, at] = found[k]
-        return tuple(squares[k] + found[k] * found[k] for k in range(rank))
-
-    squares = lax.fori_loop(
-        0, chunks, one_chunk, tuple(jnp.zeros((CHUNK, LANES), jnp.float32) for _ in range(rank))
-    )
+            values = slot[k * unit : (k + 1) * unit]
+            coeff_ref[k, pl.ds(i * unit, unit)] = values
+            squares[k] = squares[k] + values * values
     squares_ref[...] = jnp.concatenate(
         [jnp.broadcast_to(jnp.sum(squares[k], keepdims=True), (1, LANES)) for k in range(rank)] + filler, axis=0
     )
 
-    advance(late)
     for part in late:
         part.from_sibling()
-    for part in early + late:
+    for part in [power_part, coeff_part] + late:
         part.drain()
-
-
-def apply_kernel(scale, rank, rows_local, ortho_ref, mine_ref, squares_ref, x_ref, w_all_ref, coeff_ref, m_ref, g_ref,
+    for copy in [copy_c, copy_x, copy_y] + copy_z:
+        copy.wait_send()
+
+
+def apply_kernel(scale, rank, rows_local, ortho_ref, mine_ref, squares_ref, x_ref, w_all_ref, coeff_ref, buffer_ref,
                  w_ref, act_ref, nm_ref, nb_ref, nw_ref, spread):
     rows = w_all_ref.shape[0]
     coeff = [coeff_ref[k] for k in range(rank)]
@@ -271,13 +326,16 @@
         feedback = mine_ref[pl.ds(row * SUB, 1)] * coeff[0]
         for k in range(1, rank):
             feedback = feedback + mine_ref[pl.ds(row * SUB + k, 1)] * coeff[k]
-        nm_ref[row] = decay_rate * m_ref[row] + g_ref[row] - (1.0 - decay_rate) * feedback
+        nm_ref[row] = buffer_ref[row] - (1.0 - decay_rate) * feedback
     for row in range(rows):
-        spread[pl.ds(row * CHUNK, CHUNK)] = lowered(w_all_ref[row], ortho_ref, row)
-    weights = jnp.concatenate(
-        [spread[pl.ds(j, rows, stride=CHUNK)].astype(jnp.bfloat16) for j in range(CHUNK)], axis=1
-    )
-    act_ref[...] = jnp.dot(x_ref[...], weights, preferred_element_type=jnp.float32).astype(jnp.bfloat16)
+        spread[pl.ds(row * PITCH, CHUNK)] = lowered(w_all_ref[row], ortho_ref, row)
+    for j in range(0, CHUNK, 2):
+        weights = jnp.concatenate(
+            [spread[pl.ds(j + i, rows, stride=PITCH)].astype(jnp.bfloat16) for i in range(2)], axis=1
+        )
+        act_ref[:, pl.ds(j * LANES, 2 * LANES)] = jnp.dot(
+            x_ref[...], weights, preferred_element_type=jnp.float32
+        ).astype(jnp.bfloat16)
 
 
 def on_device(fsdp, tp, momentum, gradient, basis, weight, inputs):
@@ -311,32 +369,49 @@
         power = jnp.zeros((SUB, LANES), jnp.float32)
 
     vmem = pl.BlockSpec(memory_space=pltpu.VMEM)
+    hbm = pl.BlockSpec(memory_space=pltpu.HBM)
     anywhere = pl.BlockSpec(memory_space=pl.ANY)
-    parts = 1 + len(split_chunks(BUFFER_PLAN, chunks)) + len(split_chunks(WEIGHT_PLAN, chunks))
+    unit = SUB * -(-groups // (SUB * fsdp))
+    assert groups % unit == 0
+    parts = 2 + len(split_chunks(WEIGHT_PLAN, chunks))
     f32, bf16 = jnp.float32, jnp.bfloat16
-    gathered, coeff, ortho, mine, squares = pl.pallas_call(
-        functools.partial(gather_kernel, depth, rank, rows_local, tp > 1),
+    slot = (rank * unit, LANES)
+    gathered, coeff, buffer, x, ortho, mine, squares = pl.pallas_call(
+        functools.partial(gather_kernel, depth, rank, rows_local, unit, tp > 1),
         out_shape=(
             jax.ShapeDtypeStruct((depth, 2, 2, 2, rows_local, groups, LANES), bf16),
             jax.ShapeDtypeStruct((rank, groups, LANES), f32),
+            jax.ShapeDtypeStruct((rows_local, groups, LANES), f32),
+            jax.ShapeDtypeStruct((tokens, rows), bf16),
             jax.ShapeDtypeStruct((rows * SUB, LANES), f32),
             jax.ShapeDtypeStruct((rows_local * SUB, LANES), f32),
             jax.ShapeDtypeStruct((SUB, LANES), f32),
         ),
-        in_specs=[vmem] * 5,
-        out_specs=(anywhere, vmem, vmem, vmem, vmem),
+        in_specs=[hbm] * 4 + [vmem] * 2,
+        out_specs=(anywhere,) + (vmem,) * 6,
         scratch_shapes=[
-            pltpu.VMEM((depth, 2, 2, 2, rows_local, groups, LANES), bf16),
+            pltpu.VMEM(m.shape, f32),
+            pltpu.VMEM(g.shape, f32),
+            pltpu.VMEM(b.shape, f32),
+            pltpu.VMEM((rows, tokens), bf16),
+            pltpu.VMEM((depth, 2, 2, 2) + slot, f32),
+            pltpu.VMEM((depth, 2, 2) + slot, f32),
+            pltpu.VMEM((depth, 2) + slot, f32),
+            pltpu.VMEM((depth,) + slot, f32),
+            pltpu.VMEM((depth,) + slot, f32),
+            pltpu.VMEM((depth, 2, 2, 2) + slot, f32),
             pltpu.VMEM((depth, 2, 2, 2, rows_local * SUB, LANES), f32),
             pltpu.SemaphoreType.DMA((parts, 4 + depth)),
             pltpu.SemaphoreType.DMA((parts, 4 + depth)),
-            pltpu.SemaphoreType.DMA,
+            pltpu.SemaphoreType.DMA((2 + depth,)),
+            pltpu.SemaphoreType.DMA((2 + depth,)),
+            pltpu.SemaphoreType.DMA((5,)),
         ],
         compiler_params=pltpu.CompilerParams(
             collective_id=0, has_side_effects=True, vmem_limit_bytes=32 * 1024 * 1024
         ),
         name="gather_rows",
-    )(m, g, b, w, power)
+    )(m, g, b, inputs.T, w, power)
 
     if tp > 1:
         squares = lax.psum(squares, "tp")
@@ -358,8 +433,8 @@
             jax.ShapeDtypeStruct((rows_local, groups, LANES), bf16),
         ),
         in_specs=[
-            whole(ortho), whole(mine), whole(squares), whole(inputs),
-            sliced(rows), sliced(rank), sliced(rows_local), sliced(rows_local), sliced(rows_local),
+            whole(ortho), whole(mine), whole(squares), whole(x),
+            sliced(rows), sliced(rank), sliced(rows_local), sliced(rows_local),
         ],
         out_specs=(
             pl.BlockSpec((tokens, block), lambda i: (0, i)),
@@ -367,10 +442,10 @@
             pl.BlockSpec((CHUNK * rank, LANES), lambda i: (i, 0)),
             sliced(rows_local),
         ),
-        scratch_shapes=[pltpu.VMEM((rows * CHUNK, LANES), f32)],
+        scratch_shapes=[pltpu.VMEM((rows * PITCH, LANES), f32)],
         compiler_params=pltpu.CompilerParams(vmem_limit_bytes=32 * 1024 * 1024),
         name="apply_update",
-    )(ortho, mine, squares, inputs, w_all, coeff, m, g, w)
+    )(ortho, mine, squares, x, w_all, coeff, buffer, w)
 
     def flat(array):
         return array.reshape(array.shape[0], padded)[:, :width]

time: 45.6 us -> 45.2 us (level)
    unnamed x8 -> x9, local copies, waits for them, and re-layouts: 4.25 us -> 4.14 us
where the time goes in v2:
time: 45.2 us; the launch traced here: 44.9 us
  Pallas kernels  38.9 us (86%)
  local copies, waits for them, and re-layouts  4.14 us (9%)
  other arithmetic  1.19 us (3%)
  between operations  0.66 us (1%)
    pallas_call x1, Pallas kernels, on_device(): pl.pallas_call(functools.partial(gather_kernel, depth, rank, rows_local,...  30.7 us
    pallas_call x1, Pallas kernels, on_device(): pl.pallas_call(functools.partial(apply_kernel, scale, rank, rows_local),...  8.19 us
    unnamed x9, local copies, waits for them, and re-layouts  4.14 us
    unnamed x1, other arithmetic  1.19 us

profile of v2, /device:TPU:0, one launch (start us, length us, event | category | flops | bytes accessed | tf_op | source)
XLA Modules:
  0.0 44.9 jit_solution(10863367293247800886)
XLA Ops:
  0.6 1.2 %reduce = bf16[26624]{0:T(1024)(128)(2,1)S(1)} reduce(bf16[1,26624]{1,0:T(2,128)(2,1)} %param.8, bf16[]{:T(256)} %constant.5), dimensions={0}, to_apply=%param.8.reduce_sub_computation | reduce | bytes 106498 | tf_op args[3]
  1.8 0.0 copy-start
  1.8 0.9 %copy-done = f32[2,26624]{1,0:T(2,128)S(1)} copy-done((f32[2,26624]{1,0:T(2,128)S(1)}, f32[2,26624]{1,0:T(2,128)}, u32[]{:S(2)}) %copy-start) | copy-done | bytes 213016
  2.8 0.0 copy-start.1
  2.8 0.9 %copy-done.1 = f32[1,26624]{1,0:T(1,128)S(1)} copy-done((f32[1,26624]{1,0:T(1,128)S(1)}, f32[1,26624]{1,0:T(1,128)}, u32[]{:S(2)}) %copy-start.1) | copy-done | bytes 106520
  3.7 0.0 copy-start.2
  3.7 0.9 %copy-done.2 = f32[1,26624]{1,0:T(1,128)S(1)} copy-done((f32[1,26624]{1,0:T(1,128)S(1)}, f32[1,26624]{1,0:T(1,128)}, u32[]{:S(2)}) %copy-start.2) | copy-done | bytes 106520
  4.6 0.0 copy-start.3
  4.6 0.7 %copy-done.3 = bf16[128,32]{0,1:T(8,128)(2,1)S(1)} copy-done((bf16[128,32]{0,1:T(8,128)(2,1)S(1)}, bf16[128,32]{0,1:T(8,128)(2,1)}, u32[]{:S(2)}) %copy-start.3) | copy-done | bytes 8216
  5.3 30.7 %gather_rows.1 = (bf16[4,2,2,2,1,208,128]{6,5,4,3,2,1,0:T(8,128)(2,1)S(1)}, f32[2,208,128]{2,1,0:T(8,128)S(1)}, f32[1,208,128]{2,1,0:T(8,128)S(1)}, bf16[128,32]...) custom-call(f32[1,208,128]{2,1,0:T(8,128)S(1)} %bitcast.24, ...), custom_call_target="tpu_custom_call" | custom-call | tf_op jit(solution)/shard_map/gather_rows/pallas_call | solution.py:379
  36.0 8.2 %apply_update.1 = (bf16[128,26624]{1,0:T(8,128)(2,1)}, f32[1,208,128]{2,1,0:T(8,128)}, f32[416,128]{1,0:T(8,128)}, bf16[1,208,128]{2,1,0:T(8,128)(2,1)S(1)}) custom-call(f32[256,128]{1,0:T(8,128)S(1)} %get-tuple-element.15.ortho_ref, f32[8,128]{1,0:T(8,128)S(1)} %get-tuple-element.16.mine_ref, f32[8,128]{1,0:T(8,128)S(1)} %get-tuple-element.17.squares_ref, ...), custom_call_target="tpu_custom_call" | custom-call | tf_op jit(solution)/shard_map/apply_update/pallas_call | solution.py:426
  44.2 0.7 %copy.13 = bf16[1,1,208,128]{3,1,2,0:T(2,128)(2,1)} copy(bf16[1,1,208,128]{3,2,1,0:T(8,128)(2,1)S(1)} %bitcast.26) | data formatting | bytes 106496
  (1 shorter events, 0.0 us)
Async XLA Ops:
  1.8 0.9 %copy-start = (f32[2,26624]{1,0:T(2,128)S(1)}, f32[2,26624]{1,0:T(2,128)}, u32[]{:S(2)}) copy-start(f32[2,26624]{1,0:T(2,128)} %param.7) | copy-start | bytes 638980
  2.8 0.9 %copy-start.1 = (f32[1,26624]{1,0:T(1,128)S(1)}, f32[1,26624]{1,0:T(1,128)}, u32[]{:S(2)}) copy-start(f32[1,26624]{1,0:T(1,128)} %param.5) | copy-start | bytes 319492
  3.7 0.9 %copy-start.2 = (f32[1,26624]{1,0:T(1,128)S(1)}, f32[1,26624]{1,0:T(1,128)}, u32[]{:S(2)}) copy-start(f32[1,26624]{1,0:T(1,128)} %param.6) | copy-start | bytes 319492
  4.6 0.7 %copy-start.3 = (bf16[128,32]{0,1:T(8,128)(2,1)S(1)}, bf16[128,32]{0,1:T(8,128)(2,1)}, u32[]{:S(2)}) copy-start(bf16[128,32]{0,1:T(8,128)(2,1)} %param.9) | copy-start | bytes 24580

commit v3 on v2

--- a/solution.py
+++ b/solution.py
@@ -14,11 +14,12 @@
 highest = lax.Precision.HIGHEST
 MESH = pl.DeviceIdType.MESH
 LANES = 128
+PLANE = [(y, x, c) for y in range(2) for x in range(2) for c in range(2)][1:]
 CHUNK = 16
 PITCH = 24
 SUB = 8
 
-WEIGHT_PLAN = (("yzx", 4), ("xzy", 4), ("zxy", 3), ("zyx", 2))
+WEIGHT_PLAN = (("yzx", 3), ("xzy", 3), ("zxy", 4), ("zyx", 3))
 
 
 def split_chunks(plan, chunks):
@@ -106,8 +107,8 @@
 
 def gather_kernel(depth, rank, rows_local, unit, has_power, *refs):
     (m_hbm, g_hbm, basis_hbm, xt_hbm, w_ref, power_ref, gathered, coeff_ref, buffer_ref, x_ref, ortho_ref, mine_ref,
-     squares_ref, m_ref, g_ref, basis_ref, xt_ref, sums, from_c, from_x, from_y, from_z, coeff_buf, power_buf,
-     send_sem, recv_sem, sums_send, sums_recv, local_sem) = refs
+     squares_ref, m_ref, g_ref, basis_ref, xt_ref, sums, from_plane, z_sums, from_z, coeff_buf, power_buf,
+     send_sem, recv_sem, local_sem) = refs
     groups = m_ref.shape[1]
     chunks = groups // CHUNK
     me = lax.axis_index("fsdp")
@@ -117,11 +118,10 @@
     def number(z, y, x, c):
         return ((z * 2 + y) * 2 + x) * 2 + c
 
-    partners = [number((coords["z"] + k) % depth, *here[1:]) for k in range(1, depth)]
-    over_y = number(here[0], 1 - here[1], here[2], here[3])
-    over_x = number(here[0], here[1], 1 - here[2], here[3])
-    sibling = number(here[0], here[1], here[2], 1 - here[3])
-    partners += [over_y, over_x, sibling]
+    z, y, x, c = here
+    peers = [((y + dy) % 2, (x + dx) % 2, (c + dc) % 2) for dy, dx, dc in PLANE]
+    partners = [number((z + k) % depth, y, x, c) for k in range(1, depth)]
+    partners += [number(z, *peer) for peer in peers]
     barrier = pltpu.get_barrier_semaphore()
     for partner in partners:
         pl.semaphore_signal(barrier, inc=1, device_id={"fsdp": partner}, device_id_type=MESH)
@@ -155,27 +155,25 @@
     owners = groups // unit
     own_power = [power_buf[here + (pl.ds(row * SUB, SUB),)] for row in range(rows_local)]
     for i, d in enumerate(devices):
+        if i >= owners:
+            sums[d] = jnp.zeros((rank * unit, LANES), jnp.bfloat16)
+            continue
+        terms = []
         for k in range(rank):
-            at = pl.ds(k * unit, unit)
-            if i >= owners:
-                sums[d + (at,)] = jnp.zeros((unit, LANES), jnp.float32)
-                continue
             term = jnp.zeros((unit, LANES), jnp.float32)
             for row in range(rows_local):
                 term = term + own_power[row][k : k + 1] * buffer_ref[row, pl.ds(i * unit, unit)]
-            sums[d + (at,)] = term
+            terms.append(term)
+        sums[d] = jnp.concatenate(terms, axis=0).astype(jnp.bfloat16)
     pl.semaphore_wait(barrier, len(partners))
 
     def mover(buf, window, order, count):
         return Mover(buf, window, order, count, coords, depth, send_sem, recv_sem)
 
-    everything = (slice(None), slice(None))
-    power_part = mover(power_buf, everything, "zxy", 0)
-    coeff_part = mover(coeff_buf, everything, "zxy", 1)
     late = []
     for order, first, count in split_chunks(WEIGHT_PLAN, chunks):
         window = (slice(None), pl.ds(first * CHUNK, count * CHUNK), slice(None))
-        late.append(mover(gathered, window, order, 2 + len(late)))
+        late.append(mover(gathered, window, order, 3 + len(late)))
 
     def advance(movers):
         for part in movers:
@@ -187,51 +185,60 @@
             else:
                 part.to_sibling(True)
 
-    def sums_copy(source, target, slot, device):
+    def move(source, target, number_of, slot, device):
         return pltpu.make_async_remote_copy(
-            src_ref=source, dst_ref=target, send_sem=sums_send.at[slot], recv_sem=sums_recv.at[slot],
-            device_id={"fsdp": device}, device_id_type=MESH,
+            src_ref=source, dst_ref=target, send_sem=send_sem.at[number_of, slot],
+            recv_sem=recv_sem.at[number_of, slot], device_id={"fsdp": device}, device_id_type=MESH,
         )
 
-    z, y, x, c = here
-    all_of = slice(None)
-    copy_c = sums_copy(sums.at[all_of, all_of, all_of, 1 - c], from_c, 0, sibling)
-    copy_x = sums_copy(sums.at[all_of, all_of, 1 - x, c], from_x, 1, over_x)
-    copy_y = sums_copy(sums.at[all_of, 1 - y, x, c], from_y, 2, over_y)
-    copy_z = [
-        sums_copy(sums.at[(z + k) % depth, y, x, c], from_z.at[k - 1], 2 + k,
-                  number((z + k) % depth, y, x, c))
-        for k in range(1, depth)
-    ]
-
-    power_part.start()
-    copy_c.start()
+    column = (slice(None), y, x, c)
+    hops_z = [((z + k) % depth, (z + depth - k) % depth) for k in range(1, depth)]
+    small = []
+
+    def begin(copies):
+        for copy in copies:
+            copy.start()
+        small.extend(copies)
+
+    def spread_z(buf, number_of):
+        begin([move(buf.at[here], buf.at[here], number_of, len(PLANE) + k, number(there, y, x, c))
+               for k, (there, _) in enumerate(hops_z)])
+
+    def spread_plane(buf, number_of):
+        for k, (_, source) in enumerate(hops_z):
+            slot = buf.at[source, y, x, c]
+            move(slot, slot, number_of, len(PLANE) + k, number(source, y, x, c)).wait_recv()
+        begin([move(buf.at[column], buf.at[column], number_of, k, number(z, *peer)) for k, peer in enumerate(peers)])
+
+    def arrived(buf, number_of):
+        for k, peer in enumerate(peers):
+            slot = buf.at[(slice(None),) + peer]
+            move(slot, slot, number_of, k, number(z, *peer)).wait_recv()
+
+    first, last = late[:2], late[2:]
+    spread_z(power_buf, 0)
+    to_plane = [move(sums.at[(slice(None),) + peer], from_plane.at[k], 2, k, number(z, *peer))
+                for k, peer in enumerate(peers)]
+    begin(to_plane)
     loads[0].wait()
     for part in late:
         part.start()
-    copy_c.wait_recv()
-    for i in range(depth):
-        for j in range(2):
-            for h in range(2):
-                sums[i, j, h, c] = sums[i, j, h, c] + from_c[i, j, h]
-    copy_x.start()
-    advance([power_part])
+    advance(first)
+    spread_plane(power_buf, 0)
     loads[4].wait()
     x_ref[...] = jnp.transpose(xt_ref[...].astype(jnp.float32)).astype(jnp.bfloat16)
-    copy_x.wait_recv()
+    for copy in to_plane:
+        copy.wait_recv()
     for i in range(depth):
-        for j in range(2):
-            sums[i, j, x, c] = sums[i, j, x, c] + from_x[i, j]
-    copy_y.start()
-    advance([power_part])
-    advance(late)
-    copy_y.wait_recv()
-    for i in range(depth):
-        sums[i, y, x, c] = sums[i, y, x, c] + from_y[i]
-    for copy in copy_z:
-        copy.start()
-    advance([power_part])
-    power_part.from_sibling()
+        total = sums[i, y, x, c].astype(jnp.float32)
+        for k in range(len(PLANE)):
+            total = total + from_plane[k, i].astype(jnp.float32)
+        z_sums[i] = total.astype(jnp.bfloat16)
+    over_z = [move(z_sums.at[there], from_z.at[k], 2, len(PLANE) + k, number(there, y, x, c))
+              for k, (there, _) in enumerate(hops_z)]
+    begin(over_z)
+    advance(last)
+    arrived(power_buf, 0)
 
     tiles = [power_buf[d + (pl.ds(row * SUB, SUB),)] for d in devices for row in range(rows_local)]
     gram = []
@@ -263,13 +270,16 @@
             found.append(value * inverse[k])
         return found
 
-    for copy in copy_z:
+    for copy in over_z:
         copy.wait_recv()
-    total = sums[here]
-    for k in range(1, depth):
-        total = total + from_z[k - 1]
-    coeff_buf[here] = jnp.concatenate(solve([total[k * unit : (k + 1) * unit] for k in range(rank)]), axis=0)
-    coeff_part.start()
+    total = z_sums[z].astype(jnp.float32)
+    for k in range(depth - 1):
+        total = total + from_z[k].astype(jnp.float32)
+    coeff_buf[here] = jnp.concatenate(
+        solve([total[k * unit : (k + 1) * unit] for k in range(rank)]), axis=0
+    ).astype(jnp.bfloat16)
+    spread_z(coeff_buf, 1)
+    advance(last)
 
     filler = [jnp.zeros((1, LANES), jnp.float32)] * (SUB - rank)
     for i, tile in enumerate(tiles):
@@ -280,15 +290,12 @@
         found = solve([tile[k : k + 1] for k in range(rank)])
         mine_ref[pl.ds(row * SUB, SUB)] = jnp.concatenate(found + filler, axis=0)
 
-    advance([coeff_part])
-    advance(late)
-    advance([coeff_part])
-    advance([coeff_part])
-    advance(late)
-    coeff_part.from_sibling()
+    spread_plane(coeff_buf, 1)
+    advance(first)
+    arrived(coeff_buf, 1)
     squares = [jnp.zeros((unit, LANES), jnp.float32) for _ in range(rank)]
     for i in range(owners):
-        slot = coeff_buf[devices[i]]
+        slot = coeff_buf[devices[i]].astype(jnp.float32)
         for k in range(rank):
             values = slot[k * unit : (k + 1) * unit]
             coeff_ref[k, pl.ds(i * unit, unit)] = values
@@ -297,45 +304,74 @@
         [jnp.broadcast_to(jnp.sum(squares[k], keepdims=True), (1, LANES)) for k in range(rank)] + filler, axis=0
     )
 
+    advance(last)
+    advance(first)
     for part in late:
         part.from_sibling()
-    for part in [power_part, coeff_part] + late:
+    for part in late:
         part.drain()
-    for copy in [copy_c, copy_x, copy_y] + copy_z:
+    for copy in small:
         copy.wait_send()
 
 
-def apply_kernel(scale, rank, rows_local, ortho_ref, mine_ref, squares_ref, x_ref, w_all_ref, coeff_ref, buffer_ref,
-                 w_ref, act_ref, nm_ref, nb_ref, nw_ref, spread):
-    rows = w_all_ref.shape[0]
-    coeff = [coeff_ref[k] for k in range(rank)]
-    basis = []
-    for k in range(rank):
-        norm = jnp.sqrt(squares_ref[k : k + 1] + epsilon)
-        basis.append(coeff[k] * (1.0 / norm))
-        nb_ref[pl.ds(k, CHUNK, stride=rank)] = basis[k]
-
-    def lowered(weight, ref, row):
-        change = ref[pl.ds(row * SUB, 1)] * basis[0]
-        for k in range(1, rank):
-            change = change + ref[pl.ds(row * SUB + k, 1)] * basis[k]
-        return weight.astype(jnp.float32) - scale * change
-
-    for row in range(rows_local):
-        nw_ref[row] = lowered(w_ref[row], mine_ref, row).astype(jnp.bfloat16)
-        feedback = mine_ref[pl.ds(row * SUB, 1)] * coeff[0]
-        for k in range(1, rank):
-            feedback = feedback + mine_ref[pl.ds(row * SUB + k, 1)] * coeff[k]
-        nm_ref[row] = buffer_ref[row] - (1.0 - decay_rate) * feedback
-    for row in range(rows):
-        spread[pl.ds(row * PITCH, CHUNK)] = lowered(w_all_ref[row], ortho_ref, row)
-    for j in range(0, CHUNK, 2):
+def apply_kernel(scale, rank, rows_local, ortho_ref, mine_ref, squares_ref, x_ref, w_hbm, coeff_ref, buffer_ref,
+                 w_ref, act_hbm, nm_ref, nb_ref, nw_ref, w_all_ref, act_ref, spread, load_sem, store_sem):
+    rows, groups = w_hbm.shape[:2]
+    chunks = groups // CHUNK
+    block = CHUNK * LANES
+    inverse = [1.0 / jnp.sqrt(squares_ref[k : k + 1] + epsilon) for k in range(rank)]
+
+    def load(i):
+        at = pl.ds(pl.multiple_of(i * CHUNK, CHUNK), CHUNK)
+        return pltpu.make_async_copy(w_hbm.at[:, at], w_all_ref.at[i], load_sem.at[i])
+
+    def store(i):
+        at = pl.ds(pl.multiple_of(i * block, block), block)
+        return pltpu.make_async_copy(act_ref.at[i % 2], act_hbm.at[:, at], store_sem.at[i % 2])
+
+    for i in range(chunks):
+        load(i).start()
+
+    def one_chunk(i, carry):
+        at = pl.ds(pl.multiple_of(i * CHUNK, CHUNK), CHUNK)
+        coeff = [coeff_ref[k, at] for k in range(rank)]
+        basis = [coeff[k] * inverse[k] for k in range(rank)]
+        for k in range(rank):
+            nb_ref[pl.ds(i * (CHUNK * rank) + k, CHUNK, stride=rank)] = basis[k]
+        scaled = [scale * basis[k] for k in range(rank)]
+
+        def lowered(weight, ref, row):
+            change = ref[pl.ds(row * SUB, 1)] * scaled[0]
+            for k in range(1, rank):
+                change = change + ref[pl.ds(row * SUB + k, 1)] * scaled[k]
+            return weight.astype(jnp.float32) - change
+
+        for row in range(rows_local):
+            nw_ref[row, at] = lowered(w_ref[row, at], mine_ref, row).astype(jnp.bfloat16)
+            feedback = mine_ref[pl.ds(row * SUB, 1)] * coeff[0]
+            for k in range(1, rank):
+                feedback = feedback + mine_ref[pl.ds(row * SUB + k, 1)] * coeff[k]
+            nm_ref[row, at] = buffer_ref[row, at] - (1.0 - decay_rate) * feedback
+        load(i).wait()
+        for row in range(rows):
+            spread[pl.ds(row * PITCH, CHUNK)] = lowered(w_all_ref[i, row], ortho_ref, row)
+
+        @pl.when(i >= 2)
+        def _():
+            store(i - 2).wait()
+
         weights = jnp.concatenate(
-            [spread[pl.ds(j + i, rows, stride=PITCH)].astype(jnp.bfloat16) for i in range(2)], axis=1
+            [spread[pl.ds(j, rows, stride=PITCH)].astype(jnp.bfloat16) for j in range(CHUNK)], axis=1
         )
-        act_ref[:, pl.ds(j * LANES, 2 * LANES)] = jnp.dot(
+        act_ref[i % 2] = jnp.dot(
             x_ref[...], weights, preferred_element_type=jnp.float32
         ).astype(jnp.bfloat16)
+        store(i).start()
+        return carry
+
+    lax.fori_loop(0, chunks, one_chunk, 0)
+    for i in range(max(chunks - 2, 0), chunks):
+        store(i).wait()
 
 
 def on_device(fsdp, tp, momentum, gradient, basis, weight, inputs):
@@ -373,7 +409,7 @@
     anywhere = pl.BlockSpec(memory_space=pl.ANY)
     unit = SUB * -(-groups // (SUB * fsdp))
     assert groups % unit == 0
-    parts = 2 + len(split_chunks(WEIGHT_PLAN, chunks))
+    parts = 3 + len(split_chunks(WEIGHT_PLAN, chunks))
     f32, bf16 = jnp.float32, jnp.bfloat16
     slot = (rank * unit, LANES)
     gathered, coeff, buffer, x, ortho, mine, squares = pl.pallas_call(
@@ -394,21 +430,18 @@
             pltpu.VMEM(g.shape, f32),
             pltpu.VMEM(b.shape, f32),
             pltpu.VMEM((rows, tokens), bf16),
-            pltpu.VMEM((depth, 2, 2, 2) + slot, f32),
-            pltpu.VMEM((depth, 2, 2) + slot, f32),
-            pltpu.VMEM((depth, 2) + slot, f32),
-            pltpu.VMEM((depth,) + slot, f32),
-            pltpu.VMEM((depth,) + slot, f32),
-            pltpu.VMEM((depth, 2, 2, 2) + slot, f32),
+            pltpu.VMEM((depth, 2, 2, 2) + slot, bf16),
+            pltpu.VMEM((len(PLANE), depth) + slot, bf16),
+            pltpu.VMEM((depth,) + slot, bf16),
+            pltpu.VMEM((depth,) + slot, bf16),
+            pltpu.VMEM((depth, 2, 2, 2) + slot, bf16),
             pltpu.VMEM((depth, 2, 2, 2, rows_local * SUB, LANES), f32),
-            pltpu.SemaphoreType.DMA((parts, 4 + depth)),
-            pltpu.SemaphoreType.DMA((parts, 4 + depth)),
-            pltpu.SemaphoreType.DMA((2 + depth,)),
-            pltpu.SemaphoreType.DMA((2 + depth,)),
+            pltpu.SemaphoreType.DMA((parts, len(PLANE) + depth)),
+            pltpu.SemaphoreType.DMA((parts, len(PLANE) + depth)),
             pltpu.SemaphoreType.DMA((5,)),
         ],
         compiler_params=pltpu.CompilerParams(
-            collective_id=0, has_side_effects=True, vmem_limit_bytes=32 * 1024 * 1024
+            collective_id=0, has_side_effects=True, vmem_limit_bytes=63 * 1024 * 1024
         ),
         name="gather_rows",
     )(m, g, b, inputs.T, w, power)
@@ -417,33 +450,24 @@
         squares = lax.psum(squares, "tp")
     w_all = gathered.reshape(rows, groups, LANES)
 
-    def whole(array):
-        return pl.BlockSpec(array.shape, lambda i: (0,) * array.ndim)
-
-    def sliced(lead):
-        return pl.BlockSpec((lead, CHUNK, LANES), lambda i: (0, i, 0))
-
     act, nm, nb, nw = pl.pallas_call(
         functools.partial(apply_kernel, scale, rank, rows_local),
-        grid=(chunks,),
         out_shape=(
             jax.ShapeDtypeStruct((tokens, padded), bf16),
             jax.ShapeDtypeStruct((rows_local, groups, LANES), f32),
             jax.ShapeDtypeStruct((groups * rank, LANES), f32),
             jax.ShapeDtypeStruct((rows_local, groups, LANES), bf16),
         ),
-        in_specs=[
-            whole(ortho), whole(mine), whole(squares), whole(x),
-            sliced(rows), sliced(rank), sliced(rows_local), sliced(rows_local),
+        in_specs=[vmem] * 4 + [anywhere] + [vmem] * 3,
+        out_specs=(anywhere, vmem, vmem, vmem),
+        scratch_shapes=[
+            pltpu.VMEM((chunks, rows, CHUNK, LANES), bf16),
+            pltpu.VMEM((2, tokens, block), bf16),
+            pltpu.VMEM((rows * PITCH, LANES), f32),
+            pltpu.SemaphoreType.DMA((chunks,)),
+            pltpu.SemaphoreType.DMA((2,)),
         ],
-        out_specs=(
-            pl.BlockSpec((tokens, block), lambda i: (0, i)),
-            sliced(rows_local),
-            pl.BlockSpec((CHUNK * rank, LANES), lambda i: (i, 0)),
-            sliced(rows_local),
-        ),
-        scratch_shapes=[pltpu.VMEM((rows * PITCH, LANES), f32)],
-        compiler_params=pltpu.CompilerParams(vmem_limit_bytes=32 * 1024 * 1024),
+        compiler_params=pltpu.CompilerParams(vmem_limit_bytes=63 * 1024 * 1024),
         name="apply_update",
     )(ortho, mine, squares, x, w_all, coeff, buffer, w)
 

time: 45.2 us -> 42.9 us (0.949)
  local copies, waits for them, and re-layouts: 4.14 us -> 2.13 us
  Pallas kernels: 38.9 us -> 38 us
  other arithmetic: 1.19 us -> 1.81 us
    pallas_call x1, Pallas kernels: 30.7 us -> 27.6 us  [on_device(): pl.pallas_call(functools.partial(gather_kernel, depth, rank, rows_local,...]
    unnamed x9 -> x1, local copies, waits for them, and re-layouts: 4.14 us -> 1.53 us
    pallas_call x1, Pallas kernels: 8.19 us -> 10.4 us  [on_device(): pl.pallas_call(functools.partial(apply_kernel, scale, rank, rows_local),...]
    unnamed x1, other arithmetic: 1.19 us -> 1.81 us
    broadcast_in_dim x1, local copies, waits for them, and re-layouts: 0.01 us -> 0.59 us  [on_device(): power = jnp.zeros((SUB, LANES), jnp.float32)]
where the time goes in v3:
time: 42.9 us; the launch traced here: 42.6 us
  Pallas kernels  38 us (89%)
  local copies, waits for them, and re-layouts  2.13 us (5%)
  other arithmetic  1.81 us (4%)
  between operations  0.65 us (2%)
    pallas_call x1, Pallas kernels, on_device(): pl.pallas_call(functools.partial(gather_kernel, depth, rank, rows_local,...  27.6 us
    pallas_call x1, Pallas kernels, on_device(): pl.pallas_call(functools.partial(apply_kernel, scale, rank, rows_local),...  10.4 us
    unnamed x1, other arithmetic  1.81 us
    unnamed x1, local copies, waits for them, and re-layouts  1.53 us

profile of v3, /device:TPU:0, one launch (start us, length us, event | category | flops | bytes accessed | tf_op | source)
XLA Modules:
  0.0 42.6 jit_solution(10353273384591792276)
XLA Ops:
  0.6 1.8 %reduce = bf16[26624]{0:T(1024)(128)(2,1)} reduce(bf16[1,26624]{1,0:T(2,128)(2,1)} %param.8, bf16[]{:T(256)} %constant.5), dimensions={0}, to_apply=%param.8.reduce_sub_computation | reduce | bytes 106498 | tf_op args[3]
  2.4 0.6 %broadcast_in_dim.3.refs_5_ = f32[8,128]{1,0:T(8,128)} broadcast(f32[]{:T(128)} %constant.0.clone.1), dimensions={} | broadcast | bytes 4100 | tf_op jit(solution)/shard_map/broadcast_in_dim | solution.py:405
  3.0 27.6 %gather_rows.1 = (bf16[4,2,2,2,1,208,128]{6,5,4,3,2,1,0:T(8,128)(2,1)}, f32[2,208,128]{2,1,0:T(8,128)}, f32[1,208,128]{2,1,0:T(8,128)}, bf16[128,32]{1,0:T(8,128...) custom-call(f32[1,208,128]{2,1,0:T(8,128)} %bitcast.25, f32[1,208,128]{2,1,0:T(8,128)} %bitcast.26, ...), custom_call_target="tpu_custom_call" | custom-call | tf_op jit(solution)/shard_map/gather_rows/pallas_call | solution.py:415
  30.7 10.4 %apply_update.1 = (bf16[128,26624]{1,0:T(8,128)(2,1)}, f32[1,208,128]{2,1,0:T(8,128)}, f32[416,128]{1,0:T(8,128)}, bf16[1,208,128]{2,1,0:T(8,128)(2,1)}) custom-call(f32[256,128]{1,0:T(8,128)} %get-tuple-element.15.ortho_ref, f32[8,128]{1,0:T(8,128)} %get-tuple-element.16.mine_ref, f32[8,128]{1,0:T(8,128)} %get-tuple-element.17.squares_ref, ...), custom_call_target="tpu_custom_call" | custom-call | tf_op jit(solution)/shard_map/apply_update/pallas_call | solution.py:453
  41.0 1.5 %copy.13 = bf16[1,1,208,128]{3,1,2,0:T(2,128)(2,1)} copy(bf16[1,1,208,128]{3,2,1,0:T(8,128)(2,1)} %bitcast.27) | data formatting | bytes 106496

commit v4 on v3

--- a/solution.py
+++ b/solution.py
@@ -106,9 +106,9 @@
 
 
 def gather_kernel(depth, rank, rows_local, unit, has_power, *refs):
-    (m_hbm, g_hbm, basis_hbm, xt_hbm, w_ref, power_ref, gathered, coeff_ref, buffer_ref, x_ref, ortho_ref, mine_ref,
-     squares_ref, m_ref, g_ref, basis_ref, xt_ref, sums, from_plane, z_sums, from_z, coeff_buf, power_buf,
-     send_sem, recv_sem, local_sem) = refs
+    (m_hbm, g_hbm, basis_hbm, xt_hbm, w_ref, power_ref, wide_hbm, coeff_ref, buffer_ref, x_ref, ortho_ref, mine_ref,
+     squares_ref, gathered, wide, spread, m_ref, g_ref, basis_ref, xt_ref, sums, from_plane, z_sums, from_z, coeff_buf, power_buf,
+     send_sem, recv_sem, local_sem, wide_sem) = refs
     groups = m_ref.shape[1]
     chunks = groups // CHUNK
     me = lax.axis_index("fsdp")
@@ -129,12 +129,26 @@
     loads = [
         pltpu.make_async_copy(source, target, local_sem.at[i])
         for i, (source, target) in enumerate(
-            ((w_ref, gathered.at[here]), (m_hbm, m_ref), (g_hbm, g_ref), (basis_hbm, basis_ref), (xt_hbm, xt_ref))
+            ((m_hbm, m_ref), (g_hbm, g_ref), (basis_hbm, basis_ref), (xt_hbm, xt_ref))
         )
     ]
     for load in loads:
         load.start()
-    for load in loads[1:4]:
+    gathered[here] = w_ref[...]
+
+    def mover(buf, window, order, count):
+        return Mover(buf, window, order, count, coords, depth, send_sem, recv_sem)
+
+    late = []
+    pieces = split_chunks(WEIGHT_PLAN, chunks)
+    for order, start, count in pieces:
+        window = (slice(None), pl.ds(start * CHUNK, count * CHUNK), slice(None))
+        late.append(mover(gathered, window, order, 3 + len(late)))
+
+    pl.semaphore_wait(barrier, len(partners))
+    for part in late:
+        part.start()
+    for load in loads[:3]:
         load.wait()
 
     for row in range(rows_local):
@@ -156,7 +170,7 @@
     own_power = [power_buf[here + (pl.ds(row * SUB, SUB),)] for row in range(rows_local)]
     for i, d in enumerate(devices):
         if i >= owners:
-            sums[d] = jnp.zeros((rank * unit, LANES), jnp.bfloat16)
+            sums[d] = jnp.zeros((rank * unit, LANES), jnp.float32)
             continue
         terms = []
         for k in range(rank):
@@ -164,16 +178,7 @@
             for row in range(rows_local):
                 term = term + own_power[row][k : k + 1] * buffer_ref[row, pl.ds(i * unit, unit)]
             terms.append(term)
-        sums[d] = jnp.concatenate(terms, axis=0).astype(jnp.bfloat16)
-    pl.semaphore_wait(barrier, len(partners))
-
-    def mover(buf, window, order, count):
-        return Mover(buf, window, order, count, coords, depth, send_sem, recv_sem)
-
-    late = []
-    for order, first, count in split_chunks(WEIGHT_PLAN, chunks):
-        window = (slice(None), pl.ds(first * CHUNK, count * CHUNK), slice(None))
-        late.append(mover(gathered, window, order, 3 + len(late)))
+        sums[d] = jnp.concatenate(terms, axis=0)
 
     def advance(movers):
         for part in movers:
@@ -220,20 +225,17 @@
     to_plane = [move(sums.at[(slice(None),) + peer], from_plane.at[k], 2, k, number(z, *peer))
                 for k, peer in enumerate(peers)]
     begin(to_plane)
-    loads[0].wait()
-    for part in late:
-        part.start()
     advance(first)
     spread_plane(power_buf, 0)
-    loads[4].wait()
+    loads[3].wait()
     x_ref[...] = jnp.transpose(xt_ref[...].astype(jnp.float32)).astype(jnp.bfloat16)
     for copy in to_plane:
         copy.wait_recv()
     for i in range(depth):
-        total = sums[i, y, x, c].astype(jnp.float32)
+        total = sums[i, y, x, c]
         for k in range(len(PLANE)):
-            total = total + from_plane[k, i].astype(jnp.float32)
-        z_sums[i] = total.astype(jnp.bfloat16)
+            total = total + from_plane[k, i]
+        z_sums[i] = total
     over_z = [move(z_sums.at[there], from_z.at[k], 2, len(PLANE) + k, number(there, y, x, c))
               for k, (there, _) in enumerate(hops_z)]
     begin(over_z)
@@ -272,9 +274,9 @@
 
     for copy in over_z:
         copy.wait_recv()
-    total = z_sums[z].astype(jnp.float32)
+    total = z_sums[z]
     for k in range(depth - 1):
-        total = total + from_z[k].astype(jnp.float32)
+        total = total + from_z[k]
     coeff_buf[here] = jnp.concatenate(
         solve([total[k * unit : (k + 1) * unit] for k in range(rank)]), axis=0
     ).astype(jnp.bfloat16)
@@ -305,25 +307,58 @@
     )
 
     advance(last)
-    advance(first)
-    for part in late:
+
+    rows = len(devices) * rows_local
+
+    def relay(number):
+        part, (_, start, count) = late[number], pieces[number]
         part.from_sibling()
+
+        def one_chunk(i, carry):
+            at = pl.ds(pl.multiple_of(i * CHUNK, CHUNK), CHUNK)
+            for place, d in enumerate(devices):
+                for row in range(rows_local):
+                    spread[pl.ds((place * rows_local + row) * PITCH, CHUNK)] = gathered[d + (row, at)].astype(
+                        jnp.float32
+                    )
+            for j in range(CHUNK):
+                wide[i, pl.ds(j * rows, rows)] = spread[pl.ds(j, rows, stride=PITCH)].astype(jnp.bfloat16)
+            return carry
+
+        lax.fori_loop(start, start + count, one_chunk, 0)
+        copy = pltpu.make_async_copy(
+            wide.at[pl.ds(start, count)], wide_hbm.at[pl.ds(start, count)], wide_sem.at[number]
+        )
+        copy.start()
+        return copy
+
+    copies = []
+    if len(late) <= 2:
+        advance(first)
+    for number in range(2, len(late)):
+        copies.append(relay(number))
+        if number == 2:
+            advance(first)
+    for number in range(min(2, len(late))):
+        copies.append(relay(number))
+    for copy in copies:
+        copy.wait()
     for part in late:
         part.drain()
     for copy in small:
         copy.wait_send()
 
 
-def apply_kernel(scale, rank, rows_local, ortho_ref, mine_ref, squares_ref, x_ref, w_hbm, coeff_ref, buffer_ref,
-                 w_ref, act_hbm, nm_ref, nb_ref, nw_ref, w_all_ref, act_ref, spread, load_sem, store_sem):
-    rows, groups = w_hbm.shape[:2]
-    chunks = groups // CHUNK
+def apply_kernel(scale, rank, rows_local, ortho_ref, mine_ref, squares_ref, x_ref, wide_hbm, coeff_ref, buffer_ref,
+                 w_ref, act_hbm, nm_ref, nb_ref, nw_ref, wide, act_ref, load_sem, store_sem):
+    chunks = wide_hbm.shape[0]
+    rows = wide_hbm.shape[1] // CHUNK
     block = CHUNK * LANES
+    ortho = [ortho_ref[pl.ds(k, rows, stride=SUB)] for k in range(rank)]
     inverse = [1.0 / jnp.sqrt(squares_ref[k : k + 1] + epsilon) for k in range(rank)]
 
     def load(i):
-        at = pl.ds(pl.multiple_of(i * CHUNK, CHUNK), CHUNK)
-        return pltpu.make_async_copy(w_hbm.at[:, at], w_all_ref.at[i], load_sem.at[i])
+        return pltpu.make_async_copy(wide_hbm.at[i], wide.at[i], load_sem.at[i])
 
     def store(i):
         at = pl.ds(pl.multiple_of(i * block, block), block)
@@ -353,16 +388,19 @@
                 feedback = feedback + mine_ref[pl.ds(row * SUB + k, 1)] * coeff[k]
             nm_ref[row, at] = buffer_ref[row, at] - (1.0 - decay_rate) * feedback
         load(i).wait()
-        for row in range(rows):
-            spread[pl.ds(row * PITCH, CHUNK)] = lowered(w_all_ref[i, row], ortho_ref, row)
+        tiles = []
+        for j in range(CHUNK):
+            change = ortho[0] * scaled[0][j : j + 1]
+            for k in range(1, rank):
+                change = change + ortho[k] * scaled[k][j : j + 1]
+            tile = wide[i, pl.ds(j * rows, rows)].astype(jnp.float32) - change
+            tiles.append(tile.astype(jnp.bfloat16))
 
         @pl.when(i >= 2)
         def _():
             store(i - 2).wait()
 
-        weights = jnp.concatenate(
-            [spread[pl.ds(j, rows, stride=PITCH)].astype(jnp.bfloat16) for j in range(CHUNK)], axis=1
-        )
+        weights = jnp.concatenate(tiles, axis=1)
         act_ref[i % 2] = jnp.dot(
             x_ref[...], weights, preferred_element_type=jnp.float32
         ).astype(jnp.bfloat16)
@@ -402,7 +440,7 @@
         power = jnp.pad(power, ((0, 0), (0, SUB - rank))).reshape(rows_local * SUB, 1)
         power = jnp.broadcast_to(power, (rows_local * SUB, LANES))
     else:
-        power = jnp.zeros((SUB, LANES), jnp.float32)
+        power = inputs.T
 
     vmem = pl.BlockSpec(memory_space=pltpu.VMEM)
     hbm = pl.BlockSpec(memory_space=pltpu.HBM)
@@ -412,10 +450,10 @@
     parts = 3 + len(split_chunks(WEIGHT_PLAN, chunks))
     f32, bf16 = jnp.float32, jnp.bfloat16
     slot = (rank * unit, LANES)
-    gathered, coeff, buffer, x, ortho, mine, squares = pl.pallas_call(
+    wide, coeff, buffer, x, ortho, mine, squares = pl.pallas_call(
         functools.partial(gather_kernel, depth, rank, rows_local, unit, tp > 1),
         out_shape=(
-            jax.ShapeDtypeStruct((depth, 2, 2, 2, rows_local, groups, LANES), bf16),
+            jax.ShapeDtypeStruct((chunks, CHUNK * rows, LANES), bf16),
             jax.ShapeDtypeStruct((rank, groups, LANES), f32),
             jax.ShapeDtypeStruct((rows_local, groups, LANES), f32),
             jax.ShapeDtypeStruct((tokens, rows), bf16),
@@ -423,22 +461,26 @@
             jax.ShapeDtypeStruct((rows_local * SUB, LANES), f32),
             jax.ShapeDtypeStruct((SUB, LANES), f32),
         ),
-        in_specs=[hbm] * 4 + [vmem] * 2,
+        in_specs=[hbm] * 4 + [vmem, vmem if tp > 1 else hbm],
         out_specs=(anywhere,) + (vmem,) * 6,
         scratch_shapes=[
+            pltpu.VMEM((depth, 2, 2, 2, rows_local, groups, LANES), bf16),
+            pltpu.VMEM((chunks, CHUNK * rows, LANES), bf16),
+            pltpu.VMEM((rows * PITCH, LANES), f32),
             pltpu.VMEM(m.shape, f32),
             pltpu.VMEM(g.shape, f32),
             pltpu.VMEM(b.shape, f32),
             pltpu.VMEM((rows, tokens), bf16),
-            pltpu.VMEM((depth, 2, 2, 2) + slot, bf16),
-            pltpu.VMEM((len(PLANE), depth) + slot, bf16),
-            pltpu.VMEM((depth,) + slot, bf16),
-            pltpu.VMEM((depth,) + slot, bf16),
+            pltpu.VMEM((depth, 2, 2, 2) + slot, f32),
+            pltpu.VMEM((len(PLANE), depth) + slot, f32),
+            pltpu.VMEM((depth,) + slot, f32),
+            pltpu.VMEM((depth,) + slot, f32),
             pltpu.VMEM((depth, 2, 2, 2) + slot, bf16),
             pltpu.VMEM((depth, 2, 2, 2, rows_local * SUB, LANES), f32),
             pltpu.SemaphoreType.DMA((parts, len(PLANE) + depth)),
             pltpu.SemaphoreType.DMA((parts, len(PLANE) + depth)),
-            pltpu.SemaphoreType.DMA((5,)),
+            pltpu.SemaphoreType.DMA((4,)),
+            pltpu.SemaphoreType.DMA((parts,)),
         ],
         compiler_params=pltpu.CompilerParams(
             collective_id=0, has_side_effects=True, vmem_limit_bytes=63 * 1024 * 1024
@@ -448,7 +490,6 @@
 
     if tp > 1:
         squares = lax.psum(squares, "tp")
-    w_all = gathered.reshape(rows, groups, LANES)
 
     act, nm, nb, nw = pl.pallas_call(
         functools.partial(apply_kernel, scale, rank, rows_local),
@@ -461,15 +502,14 @@
         in_specs=[vmem] * 4 + [anywhere] + [vmem] * 3,
         out_specs=(anywhere, vmem, vmem, vmem),
         scratch_shapes=[
-            pltpu.VMEM((chunks, rows, CHUNK, LANES), bf16),
+            pltpu.VMEM((chunks, CHUNK * rows, LANES), bf16),
             pltpu.VMEM((2, tokens, block), bf16),
-            pltpu.VMEM((rows * PITCH, LANES), f32),
             pltpu.SemaphoreType.DMA((chunks,)),
             pltpu.SemaphoreType.DMA((2,)),
         ],
         compiler_params=pltpu.CompilerParams(vmem_limit_bytes=63 * 1024 * 1024),
         name="apply_update",
-    )(ortho, mine, squares, x, w_all, coeff, buffer, w)
+    )(ortho, mine, squares, x, wide, coeff, buffer, w)
 
     def flat(array):
         return array.reshape(array.shape[0], padded)[:, :width]

time: 42.9 us -> 44 us (1.026)
  Pallas kernels: 38 us -> 39.8 us
  local copies, waits for them, and re-layouts: 2.13 us -> 1.53 us
    pallas_call x1, Pallas kernels: 27.6 us -> 29.5 us  [on_device(): pl.pallas_call(functools.partial(gather_kernel, depth, rank, rows_local,...]
    broadcast_in_dim x1 -> x0, local copies, waits for them, and re-layouts: 0.59 us -> none  [on_device(): power = jnp.zeros((SUB, LANES), jnp.float32)]
where the time goes in v4:
time: 44 us; the launch traced here: 43.7 us
  Pallas kernels  39.8 us (90%)
  other arithmetic  1.81 us (4%)
  local copies, waits for them, and re-layouts  1.53 us (3%)
  between operations  0.65 us (1%)
    pallas_call x1, Pallas kernels, on_device(): pl.pallas_call(functools.partial(gather_kernel, depth, rank, rows_local,...  29.5 us
    pallas_call x1, Pallas kernels, on_device(): pl.pallas_call(functools.partial(apply_kernel, scale, rank, rows_local),...  10.3 us
    unnamed x1, other arithmetic  1.81 us
    unnamed x1, local copies, waits for them, and re-layouts  1.53 us

profile of v4, /device:TPU:0, one launch (start us, length us, event | category | flops | bytes accessed | tf_op | source)
XLA Modules:
  0.0 43.7 jit_solution(13053690642542373302)
XLA Ops:
  0.6 1.8 %reduce = bf16[26624]{0:T(1024)(128)(2,1)} reduce(bf16[1,26624]{1,0:T(2,128)(2,1)} %param.8, bf16[]{:T(256)} %constant.3), dimensions={0}, to_apply=%param.8.reduce_sub_computation | reduce | bytes 106498 | tf_op args[3]
  2.4 29.5 %gather_rows.1 = (bf16[13,512,128]{2,1,0:T(8,128)(2,1)}, f32[2,208,128]{2,1,0:T(8,128)}, f32[1,208,128]{2,1,0:T(8,128)}, bf16[128,32]{1,0:T(8,128)(2,1)}, f32[25...) custom-call(f32[1,208,128]{2,1,0:T(8,128)} %bitcast.23, f32[1,208,128]{2,1,0:T(8,128)} %bitcast.24, ...), custom_call_target="tpu_custom_call" | custom-call | tf_op jit(solution)/shard_map/gather_rows/pallas_call | solution.py:453
  31.9 10.3 %apply_update.1 = (bf16[128,26624]{1,0:T(8,128)(2,1)}, f32[1,208,128]{2,1,0:T(8,128)}, f32[416,128]{1,0:T(8,128)}, bf16[1,208,128]{2,1,0:T(8,128)(2,1)}) custom-call(f32[256,128]{1,0:T(8,128)} %get-tuple-element.15.ortho_ref, f32[8,128]{1,0:T(8,128)} %get-tuple-element.16.mine_ref, f32[8,128]{1,0:T(8,128)} %get-tuple-element.17.squares_ref, ...), custom_call_target="tpu_custom_call" | custom-call | tf_op jit(solution)/shard_map/apply_update/pallas_call | solution.py:494
  42.2 1.5 %copy.13 = bf16[1,1,208,128]{3,1,2,0:T(2,128)(2,1)} copy(bf16[1,1,208,128]{3,2,1,0:T(8,128)(2,1)} %bitcast.25) | data formatting | bytes 106496

commit v5 on v4

--- a/solution.py
+++ b/solution.py
@@ -228,7 +228,16 @@
     advance(first)
     spread_plane(power_buf, 0)
     loads[3].wait()
-    x_ref[...] = jnp.transpose(xt_ref[...].astype(jnp.float32)).astype(jnp.bfloat16)
+    tokens = xt_ref.shape[1]
+    features = jnp.transpose(xt_ref[...].astype(jnp.float32)).astype(jnp.bfloat16)
+    for b in range(x_ref.shape[0] // tokens):
+        shape = (xt_ref.shape[0], x_ref.shape[1])
+        place = lax.broadcasted_iota(jnp.int32, shape, 1) == (
+            lax.broadcasted_iota(jnp.int32, shape, 0) + b * shape[0]
+        )
+        x_ref[pl.ds(b * tokens, tokens)] = jnp.dot(
+            features, jnp.where(place, 1.0, 0.0).astype(jnp.bfloat16), preferred_element_type=jnp.float32
+        ).astype(jnp.bfloat16)
     for copy in to_plane:
         copy.wait_recv()
     for i in range(depth):
@@ -400,10 +409,15 @@
         def _():
             store(i - 2).wait()
 
-        weights = jnp.concatenate(tiles, axis=1)
-        act_ref[i % 2] = jnp.dot(
-            x_ref[...], weights, preferred_element_type=jnp.float32
-        ).astype(jnp.bfloat16)
+        tokens = act_ref.shape[1]
+        stack = x_ref.shape[0] // tokens
+        pairs = [jnp.concatenate(tiles[j : j + 2], axis=1) for j in range(0, CHUNK, 2)]
+        for first in range(0, len(pairs), stack):
+            weights = jnp.concatenate(pairs[first : first + stack], axis=0)
+            for b in range(stack):
+                act_ref[i % 2, :, pl.ds((first + b) * 2 * LANES, 2 * LANES)] = jnp.dot(
+                    x_ref[pl.ds(b * tokens, tokens)], weights, preferred_element_type=jnp.float32
+                ).astype(jnp.bfloat16)
         store(i).start()
         return carry
 
@@ -450,13 +464,16 @@
     parts = 3 + len(split_chunks(WEIGHT_PLAN, chunks))
     f32, bf16 = jnp.float32, jnp.bfloat16
     slot = (rank * unit, LANES)
+    stack = 8
+    while stack > 1 and stack * rows > 2 * LANES:
+        stack //= 2
     wide, coeff, buffer, x, ortho, mine, squares = pl.pallas_call(
         functools.partial(gather_kernel, depth, rank, rows_local, unit, tp > 1),
         out_shape=(
             jax.ShapeDtypeStruct((chunks, CHUNK * rows, LANES), bf16),
             jax.ShapeDtypeStruct((rank, groups, LANES), f32),
             jax.ShapeDtypeStruct((rows_local, groups, LANES), f32),
-            jax.ShapeDtypeStruct((tokens, rows), bf16),
+            jax.ShapeDtypeStruct((stack * tokens, stack * rows), bf16),
             jax.ShapeDtypeStruct((rows * SUB, LANES), f32),
             jax.ShapeDtypeStruct((rows_local * SUB, LANES), f32),
             jax.ShapeDtypeStruct((SUB, LANES), f32),

time: 44 us -> 44.6 us (1.014)
  Pallas kernels: 39.8 us -> 40.3 us
where the time goes in v5:
time: 44.6 us; the launch traced here: 44.3 us
  Pallas kernels  40.3 us (90%)
  other arithmetic  1.81 us (4%)
  local copies, waits for them, and re-layouts  1.53 us (3%)
  between operations  0.65 us (1%)
    pallas_call x1, Pallas kernels, on_device(): pl.pallas_call(functools.partial(gather_kernel, depth, rank, rows_local,...  29.7 us
    pallas_call x1, Pallas kernels, on_device(): pl.pallas_call(functools.partial(apply_kernel, scale, rank, rows_local),...  10.7 us
    unnamed x1, other arithmetic  1.81 us
    unnamed x1, local copies, waits for them, and re-layouts  1.53 us

profile of v5, /device:TPU:0, one launch (start us, length us, event | category | flops | bytes accessed | tf_op | source)
XLA Modules:
  0.0 44.3 jit_solution(10067896917242750623)
XLA Ops:
  0.6 1.8 %reduce = bf16[26624]{0:T(1024)(128)(2,1)} reduce(bf16[1,26624]{1,0:T(2,128)(2,1)} %param.8, bf16[]{:T(256)} %constant.3), dimensions={0}, to_apply=%param.8.reduce_sub_computation | reduce | bytes 106498 | tf_op args[3]
  2.4 29.7 %gather_rows.1 = (bf16[13,512,128]{2,1,0:T(8,128)(2,1)}, f32[2,208,128]{2,1,0:T(8,128)}, f32[1,208,128]{2,1,0:T(8,128)}, bf16[1024,256]{1,0:T(8,128)(2,1)}, f32[...) custom-call(f32[1,208,128]{2,1,0:T(8,128)} %bitcast.23, f32[1,208,128]{2,1,0:T(8,128)} %bitcast.24, ...), custom_call_target="tpu_custom_call" | custom-call | tf_op jit(solution)/shard_map/gather_rows/pallas_call | solution.py:470
  32.1 10.7 %apply_update.1 = (bf16[128,26624]{1,0:T(8,128)(2,1)}, f32[1,208,128]{2,1,0:T(8,128)}, f32[416,128]{1,0:T(8,128)}, bf16[1,208,128]{2,1,0:T(8,128)(2,1)}) custom-call(f32[256,128]{1,0:T(8,128)} %get-tuple-element.15.ortho_ref, f32[8,128]{1,0:T(8,128)} %get-tuple-element.16.mine_ref, f32[8,128]{1,0:T(8,128)} %get-tuple-element.17.squares_ref, ...), custom_call_target="tpu_custom_call" | custom-call | tf_op jit(solution)/shard_map/apply_update/pallas_call | solution.py:511
  42.8 1.5 %copy.13 = bf16[1,1,208,128]{3,1,2,0:T(2,128)(2,1)} copy(bf16[1,1,208,128]{3,2,1,0:T(8,128)(2,1)} %bitcast.25) | data formatting | bytes 106496

commit v6 on v5

--- a/solution.py
+++ b/solution.py
@@ -16,6 +16,7 @@
 LANES = 128
 PLANE = [(y, x, c) for y in range(2) for x in range(2) for c in range(2)][1:]
 CHUNK = 16
+STORES = 4
 PITCH = 24
 SUB = 8
 
@@ -369,9 +370,16 @@
     def load(i):
         return pltpu.make_async_copy(wide_hbm.at[i], wide.at[i], load_sem.at[i])
 
-    def store(i):
+    share = act_ref.shape[1] // STORES
+
+    def stores(i):
         at = pl.ds(pl.multiple_of(i * block, block), block)
-        return pltpu.make_async_copy(act_ref.at[i % 2], act_hbm.at[:, at], store_sem.at[i % 2])
+        return [
+            pltpu.make_async_copy(
+                act_ref.at[i, pl.ds(q * share, share)], act_hbm.at[pl.ds(q * share, share), at], store_sem.at[i, q]
+            )
+            for q in range(STORES)
+        ]
 
     for i in range(chunks):
         load(i).start()
@@ -405,25 +413,23 @@
             tile = wide[i, pl.ds(j * rows, rows)].astype(jnp.float32) - change
             tiles.append(tile.astype(jnp.bfloat16))
 
-        @pl.when(i >= 2)
-        def _():
-            store(i - 2).wait()
-
         tokens = act_ref.shape[1]
         stack = x_ref.shape[0] // tokens
         pairs = [jnp.concatenate(tiles[j : j + 2], axis=1) for j in range(0, CHUNK, 2)]
         for first in range(0, len(pairs), stack):
             weights = jnp.concatenate(pairs[first : first + stack], axis=0)
             for b in range(stack):
-                act_ref[i % 2, :, pl.ds((first + b) * 2 * LANES, 2 * LANES)] = jnp.dot(
+                act_ref[i, :, pl.ds((first + b) * 2 * LANES, 2 * LANES)] = jnp.dot(
                     x_ref[pl.ds(b * tokens, tokens)], weights, preferred_element_type=jnp.float32
                 ).astype(jnp.bfloat16)
-        store(i).start()
+        for copy in stores(i):
+            copy.start()
         return carry
 
     lax.fori_loop(0, chunks, one_chunk, 0)
-    for i in range(max(chunks - 2, 0), chunks):
-        store(i).wait()
+    for i in range(chunks):
+        for copy in stores(i):
+            copy.wait()
 
 
 def on_device(fsdp, tp, momentum, gradient, basis, weight, inputs):
@@ -520,9 +526,9 @@
         out_specs=(anywhere, vmem, vmem, vmem),
         scratch_shapes=[
             pltpu.VMEM((chunks, CHUNK * rows, LANES), bf16),
-            pltpu.VMEM((2, tokens, block), bf16),
+            pltpu.VMEM((chunks, tokens, block), bf16),
             pltpu.SemaphoreType.DMA((chunks,)),
-            pltpu.SemaphoreType.DMA((2,)),
+            pltpu.SemaphoreType.DMA((chunks, STORES)),
         ],
         compiler_params=pltpu.CompilerParams(vmem_limit_bytes=63 * 1024 * 1024),
         name="apply_update",

time: 44.6 us -> 42.6 us (0.955)
  Pallas kernels: 40.3 us -> 38.3 us
    pallas_call x1, Pallas kernels: 10.7 us -> 8.63 us  [on_device(): pl.pallas_call(functools.partial(apply_kernel, scale, rank, rows_local),...]
where the time goes in v6:
time: 42.6 us; the launch traced here: 42.3 us
  Pallas kernels  38.3 us (90%)
  other arithmetic  1.81 us (4%)
  local copies, waits for them, and re-layouts  1.53 us (4%)
  between operations  0.65 us (2%)
    pallas_call x1, Pallas kernels, on_device(): pl.pallas_call(functools.partial(gather_kernel, depth, rank, rows_local,...  29.7 us
    pallas_call x1, Pallas kernels, on_device(): pl.pallas_call(functools.partial(apply_kernel, scale, rank, rows_local),...  8.63 us
    unnamed x1, other arithmetic  1.81 us
    unnamed x1, local copies, waits for them, and re-layouts  1.53 us

profile of v6, /device:TPU:0, one launch (start us, length us, event | category | flops | bytes accessed | tf_op | source)
XLA Modules:
  0.0 42.3 jit_solution(17683470912970628120)
XLA Ops:
  0.6 1.8 %reduce = bf16[26624]{0:T(1024)(128)(2,1)} reduce(bf16[1,26624]{1,0:T(2,128)(2,1)} %param.8, bf16[]{:T(256)} %constant.3), dimensions={0}, to_apply=%param.8.reduce_sub_computation | reduce | bytes 106498 | tf_op args[3]
  2.4 29.7 %gather_rows.1 = (bf16[13,512,128]{2,1,0:T(8,128)(2,1)}, f32[2,208,128]{2,1,0:T(8,128)}, f32[1,208,128]{2,1,0:T(8,128)}, bf16[1024,256]{1,0:T(8,128)(2,1)}, f32[...) custom-call(f32[1,208,128]{2,1,0:T(8,128)} %bitcast.23, f32[1,208,128]{2,1,0:T(8,128)} %bitcast.24, ...), custom_call_target="tpu_custom_call" | custom-call | tf_op jit(solution)/shard_map/gather_rows/pallas_call | solution.py:476
  32.1 8.6 %apply_update.1 = (bf16[128,26624]{1,0:T(8,128)(2,1)}, f32[1,208,128]{2,1,0:T(8,128)}, f32[416,128]{1,0:T(8,128)}, bf16[1,208,128]{2,1,0:T(8,128)(2,1)}) custom-call(f32[256,128]{1,0:T(8,128)} %get-tuple-element.15.ortho_ref, f32[8,128]{1,0:T(8,128)} %get-tuple-element.16.mine_ref, f32[8,128]{1,0:T(8,128)} %get-tuple-element.17.squares_ref, ...), custom_call_target="tpu_custom_call" | custom-call | tf_op jit(solution)/shard_map/apply_update/pallas_call | solution.py:517
  40.7 1.5 %copy.13 = bf16[1,1,208,128]{3,1,2,0:T(2,128)(2,1)} copy(bf16[1,1,208,128]{3,2,1,0:T(8,128)(2,1)} %bitcast.25) | data formatting | bytes 106496

commit v7 on v6

--- a/solution.py
+++ b/solution.py
@@ -107,7 +107,7 @@
 
 
 def gather_kernel(depth, rank, rows_local, unit, has_power, *refs):
-    (m_hbm, g_hbm, basis_hbm, xt_hbm, w_ref, power_ref, wide_hbm, coeff_ref, buffer_ref, x_ref, ortho_ref, mine_ref,
+    (m_hbm, g_hbm, basis_hbm, xt_hbm, w_ref, power_ref, wide_hbm, w_out, coeff_ref, buffer_ref, x_ref, ortho_ref, mine_ref,
      squares_ref, gathered, wide, spread, m_ref, g_ref, basis_ref, xt_ref, sums, from_plane, z_sums, from_z, coeff_buf, power_buf,
      send_sem, recv_sem, local_sem, wide_sem) = refs
     groups = m_ref.shape[1]
@@ -135,7 +135,13 @@
     ]
     for load in loads:
         load.start()
-    gathered[here] = w_ref[...]
+    if len(w_ref.shape) == 3:
+        w_out[...] = w_ref[...]
+    else:
+        for first in range(0, groups, CHUNK):
+            lines = [w_ref[:, pl.ds((first + j) * LANES, LANES)].astype(jnp.float32) for j in range(CHUNK)]
+            w_out[0, pl.ds(first, CHUNK)] = jnp.concatenate(lines, axis=0).astype(jnp.bfloat16)
+    gathered[here] = w_out[...]
 
     def mover(buf, window, order, count):
         return Mover(buf, window, order, count, coords, depth, send_sem, recv_sem)
@@ -399,7 +405,12 @@
             return weight.astype(jnp.float32) - change
 
         for row in range(rows_local):
-            nw_ref[row, at] = lowered(w_ref[row, at], mine_ref, row).astype(jnp.bfloat16)
+            lowered_row = lowered(w_ref[row, at], mine_ref, row)
+            if len(nw_ref.shape) == 3:
+                nw_ref[row, at] = lowered_row.astype(jnp.bfloat16)
+            else:
+                line = jnp.concatenate([lowered_row[j : j + 1] for j in range(CHUNK)], axis=1)
+                nw_ref[:, pl.ds(pl.multiple_of(i * block, block), block)] = line.astype(jnp.bfloat16)
             feedback = mine_ref[pl.ds(row * SUB, 1)] * coeff[0]
             for k in range(1, rank):
                 feedback = feedback + mine_ref[pl.ds(row * SUB + k, 1)] * coeff[k]
@@ -450,7 +461,9 @@
             array = jnp.pad(array, ((0, 0), (0, padded - width)))
         return array.reshape(array.shape[0], groups, LANES)
 
-    m, g, w = dense(momentum), dense(gradient), dense(weight)
+    as_it_lies = rows_local == 1 and padded == width
+    m, g = dense(momentum), dense(gradient)
+    w = weight if as_it_lies else dense(weight)
     b = dense(basis).transpose(1, 0, 2).reshape(groups * rank, LANES)
     if tp > 1:
         buffer = decay_rate * momentum + gradient
@@ -473,10 +486,11 @@
     stack = 8
     while stack > 1 and stack * rows > 2 * LANES:
         stack //= 2
-    wide, coeff, buffer, x, ortho, mine, squares = pl.pallas_call(
+    wide, w_dense, coeff, buffer, x, ortho, mine, squares = pl.pallas_call(
         functools.partial(gather_kernel, depth, rank, rows_local, unit, tp > 1),
         out_shape=(
             jax.ShapeDtypeStruct((chunks, CHUNK * rows, LANES), bf16),
+            jax.ShapeDtypeStruct((rows_local, groups, LANES), bf16),
             jax.ShapeDtypeStruct((rank, groups, LANES), f32),
             jax.ShapeDtypeStruct((rows_local, groups, LANES), f32),
             jax.ShapeDtypeStruct((stack * tokens, stack * rows), bf16),
@@ -485,7 +499,7 @@
             jax.ShapeDtypeStruct((SUB, LANES), f32),
         ),
         in_specs=[hbm] * 4 + [vmem, vmem if tp > 1 else hbm],
-        out_specs=(anywhere,) + (vmem,) * 6,
+        out_specs=(anywhere,) + (vmem,) * 7,
         scratch_shapes=[
             pltpu.VMEM((depth, 2, 2, 2, rows_local, groups, LANES), bf16),
             pltpu.VMEM((chunks, CHUNK * rows, LANES), bf16),
@@ -520,7 +534,7 @@
             jax.ShapeDtypeStruct((tokens, padded), bf16),
             jax.ShapeDtypeStruct((rows_local, groups, LANES), f32),
             jax.ShapeDtypeStruct((groups * rank, LANES), f32),
-            jax.ShapeDtypeStruct((rows_local, groups, LANES), bf16),
+            jax.ShapeDtypeStruct((1, width) if as_it_lies else (rows_local, groups, LANES), bf16),
         ),
         in_specs=[vmem] * 4 + [anywhere] + [vmem] * 3,
         out_specs=(anywhere, vmem, vmem, vmem),
@@ -532,13 +546,13 @@
         ],
         compiler_params=pltpu.CompilerParams(vmem_limit_bytes=63 * 1024 * 1024),
         name="apply_update",
-    )(ortho, mine, squares, x, wide, coeff, buffer, w)
+    )(ortho, mine, squares, x, wide, coeff, buffer, w_dense)
 
     def flat(array):
         return array.reshape(array.shape[0], padded)[:, :width]
 
     new_basis = flat(nb.reshape(groups, rank, LANES).transpose(1, 0, 2))
-    return flat(nm), new_basis, flat(nw), act[:, :width]
+    return flat(nm), new_basis, nw if as_it_lies else flat(nw), act[:, :width]
 
 
 def solution(mesh):

time: 42.6 us -> 39.4 us (0.925)
  other arithmetic: 1.81 us -> 0 us
  local copies, waits for them, and re-layouts: 1.53 us -> 0 us
    unnamed x1 -> x0, other arithmetic: 1.81 us -> none
    unnamed x1 -> x0, local copies, waits for them, and re-layouts: 1.53 us -> none
where the time goes in v7:
time: 39.4 us; the launch traced here: 39.2 us
  Pallas kernels  38.5 us (98%)
  between operations  0.64 us (2%)
    pallas_call x1, Pallas kernels, on_device(): pl.pallas_call(functools.partial(gather_kernel, depth, rank, rows_local,...  29.8 us
    pallas_call x1, Pallas kernels, on_device(): pl.pallas_call(functools.partial(apply_kernel, scale, rank, rows_local),...  8.76 us

profile of v7, /device:TPU:0, one launch (start us, length us, event | category | flops | bytes accessed | tf_op | source)
XLA Modules:
  0.0 39.2 jit_solution(9151726058819053963)
XLA Ops:
  0.6 29.8 %gather_rows.1 = (bf16[13,512,128]{2,1,0:T(8,128)(2,1)}, bf16[1,208,128]{2,1,0:T(8,128)(2,1)}, f32[2,208,128]{2,1,0:T(8,128)}, f32[1,208,128]{2,1,0:T(8,128)}, b...) custom-call(f32[1,208,128]{2,1,0:T(8,128)} %bitcast.15, ...), custom_call_target="tpu_custom_call" | custom-call | tf_op jit(solution)/shard_map/gather_rows/pallas_call | solution.py:489
  30.4 8.8 %apply_update.1 = (bf16[128,26624]{1,0:T(8,128)(2,1)}, f32[1,208,128]{2,1,0:T(8,128)}, f32[416,128]{1,0:T(8,128)}, bf16[1,26624]{1,0:T(2,128)(2,1)}) custom-call(f32[256,128]{1,0:T(8,128)} %get-tuple-element.16.ortho_ref, f32[8,128]{1,0:T(8,128)} %get-tuple-element.17.mine_ref, f32[8,128]{1,0:T(8,128)} %get-tuple-element.18.squares_ref, ...), custom_call_target="tpu_custom_call" | custom-call | tf_op jit(solution)/shard_map/apply_update/pallas_call | solution.py:531

commit v8 on v7

--- a/solution.py
+++ b/solution.py
@@ -20,7 +20,7 @@
 PITCH = 24
 SUB = 8
 
-WEIGHT_PLAN = (("yzx", 3), ("xzy", 3), ("zxy", 4), ("zyx", 3))
+WEIGHT_PLAN = (("yzx", 2), ("xzy", 2), ("zxy", 5), ("zyx", 4))
 
 
 def split_chunks(plan, chunks):

time: 39.4 us -> 40.5 us (1.028)
  Pallas kernels: 38.5 us -> 39.7 us
    pallas_call x1, Pallas kernels: 29.8 us -> 30.9 us  [on_device(): pl.pallas_call(functools.partial(gather_kernel, depth, rank, rows_local,...]
where the time goes in v8:
time: 40.5 us; the launch traced here: 40.3 us
  Pallas kernels  39.7 us (98%)
  between operations  0.64 us (2%)
    pallas_call x1, Pallas kernels, on_device(): pl.pallas_call(functools.partial(gather_kernel, depth, rank, rows_local,...  30.9 us
    pallas_call x1, Pallas kernels, on_device(): pl.pallas_call(functools.partial(apply_kernel, scale, rank, rows_local),...  8.75 us

profile of v8, /device:TPU:0, one launch (start us, length us, event | category | flops | bytes accessed | tf_op | source)
XLA Modules:
  0.0 40.3 jit_solution(7442027289547269656)
XLA Ops:
  0.6 30.9 %gather_rows.1 = (bf16[13,512,128]{2,1,0:T(8,128)(2,1)}, bf16[1,208,128]{2,1,0:T(8,128)(2,1)}, f32[2,208,128]{2,1,0:T(8,128)}, f32[1,208,128]{2,1,0:T(8,128)}, b...) custom-call(f32[1,208,128]{2,1,0:T(8,128)} %bitcast.15, ...), custom_call_target="tpu_custom_call" | custom-call | tf_op jit(solution)/shard_map/gather_rows/pallas_call | solution.py:489
  31.5 8.7 %apply_update.1 = (bf16[128,26624]{1,0:T(8,128)(2,1)}, f32[1,208,128]{2,1,0:T(8,128)}, f32[416,128]{1,0:T(8,128)}, bf16[1,26624]{1,0:T(2,128)(2,1)}) custom-call(f32[256,128]{1,0:T(8,128)} %get-tuple-element.16.ortho_ref, f32[8,128]{1,0:T(8,128)} %get-tuple-element.17.mine_ref, f32[8,128]{1,0:T(8,128)} %get-tuple-element.18.squares_ref, ...), custom_call_target="tpu_custom_call" | custom-call | tf_op jit(solution)/shard_map/apply_update/pallas_call | solution.py:531
